TPU v7x, 512 devices: a whole 4x4x16 slice. The times are simulated.
512 devices in a mesh: snap: 16 (over x, y), vert: 32 (over z, core).
Axes of the slice: x: 4, y: 4, z: 16, core: 2. Of those that a mesh axis runs over, the one named last changes fastest.
Arguments:
- features: bfloat16 [16, 16384, 256], P('snap', 'vert'), may hold values from -6 to 6
- tile_src: int32 [16, 1024], P('snap', 'vert'), may hold values from 0 to 127, as said below
- tile_dst: int32 [16, 1024], P('snap', 'vert'), may hold values from 0 to 127, as said below
- tile_count: int32 [16, 32], P('snap', 'vert'), may hold values from 4 to 32, as said below
- tile_vals: bfloat16 [16, 1024, 128, 128], P('snap', 'vert'), may hold values from -0.25 to 0.25
- norm_gain: float32 [256], replicated, may hold values from 0.25 to 1.75
- mix_weight: bfloat16 [256, 512], replicated, may hold values from -0.375 to 0.375
- decay_rate: float32 [16, 256], replicated, may hold values from 0 to 9, as said below
- mlp_gain: float32 [256], replicated, may hold values from 0.25 to 1.75
- up_weight: bfloat16 [256, 1024], replicated, may hold values from -0.375 to 0.375
- down_weight: bfloat16 [1024, 256], replicated, may hold values from -0.1875 to 0.1875
- link_weight: bfloat16 [256, 256], replicated, may hold values from -0.375 to 0.375
- pair_left: int32 [16, 1024], P('snap', 'vert'), may hold values from 0 to 127, as said below
- pair_right: int32 [16, 1024], P('snap', 'vert'), may hold values from 0 to 127, as said below
Outputs:
- embeddings: bfloat16 [16, 16384, 256], P('snap', 'vert')
- scores: bfloat16 [16, 1024, 128, 128], P('snap', 'vert')
Inputs may be any that keep to these rules, and one draw needn't show every extreme that they name: `tile_src`: a slot of vertex part p names a source block from p * 4 - 4 to p * 4 + 2 * 4 - 1. `tile_dst`: a slot of vertex part p names a destination block of that part, p * 4 to p * 4 + 3. `tile_count`: in every snapshot some vertex part has all 32 slots live. `decay_rate`: decay rates are positive. `pair_left`: a pair of vertex part p has its first block in that part, p * 4 to p * 4 + 3. `pair_right`: a pair of vertex part p has its second block from p * 4 - 4 to p * 4 + 2 * 4 - 1.
All inputs are finite; a program needn't handle non-finite values.
Results may differ from a plain program's by a relative error of at most 0.0091.
Values may be sent and summed in bfloat16 or wider, within the bound.
No kernel may reach another device: no remote copies, remote signals or barrier semaphores. Data moves between devices by JAX's collectives and lax.ppermute only.
A program may use at most 64 MiB of HBM per device.

v0:
```python
import jax
import jax.numpy as jnp
from jax import lax
from jax.sharding import PartitionSpec as P

epsilon = 1e-06


def with_halo(cells, sides, width):
    for axis, dim in sides:
        count = lax.axis_size(axis)
        ends = count - 1
        head = lax.slice_in_dim(cells, 0, width, axis=dim)
        tail = lax.slice_in_dim(cells, cells.shape[dim] - width, cells.shape[dim], axis=dim)
        cells = jnp.concatenate(
            [
                lax.ppermute(tail, axis, [(i, (i + 1) % count) for i in range(ends)]),
                cells,
                lax.ppermute(head, axis, [((i + 1) % count, i) for i in range(ends)]),
            ],
            axis=dim,
        )
    return cells


def root_norm(values, gain_vector):
    return (
        values
        * lax.rsqrt(jnp.mean(values * values, axis=-1, keepdims=True) + epsilon)
        * gain_vector
    )


def pick_blocks(blocks, indices):
    return jax.vmap(lambda source_table, chosen: jnp.take(source_table, chosen, axis=0))(
        blocks, indices
    )


def tile_terms(blocks, src_index, dst_index, tile_part, alive_slots, per_part):
    picked = pick_blocks(blocks, src_index)
    product = jnp.einsum("sgij,sgjf->sgif", tile_part, picked, preferred_element_type=jnp.float32)
    targets = jnp.arange(per_part, dtype=jnp.int32)[None, None, :]
    selector = ((dst_index[:, :, None] == targets) & alive_slots[:, :, None]).astype(jnp.float32)
    return jnp.einsum("sgb,sgif->sbif", selector, product, precision=lax.Precision.HIGHEST)


def gate_drive(normed, step_rates, mix_weight):
    projected = jnp.einsum("tnf,fg->tng", normed, mix_weight, preferred_element_type=jnp.float32)
    feature_width = normed.shape[-1]
    decays = jnp.exp(-step_rates[:, None, :] * jax.nn.sigmoid(projected[..., :feature_width]))
    return (decays, (1.0 - decays) * projected[..., feature_width:])


def advance(previous, inputs):
    updated = inputs[0] * previous + inputs[1]
    return (updated, updated)


def run_states(decays, drives, start_state):
    final_state, states = lax.scan(advance, start_state, (decays, drives))
    return states


def feed_forward(states, mlp_gain, up_weight, down_weight):
    state_normed = root_norm(states, mlp_gain).astype(jnp.bfloat16)
    hidden = jax.nn.silu(
        jnp.einsum("tnf,fh->tnh", state_normed, up_weight, preferred_element_type=jnp.float32)
    ).astype(jnp.bfloat16)
    return (
        states + jnp.einsum("tnh,hf->tnf", hidden, down_weight, preferred_element_type=jnp.float32)
    ).astype(jnp.bfloat16)


def body(
    features,
    tile_src,
    tile_dst,
    tile_count,
    tile_vals,
    norm_gain,
    mix_weight,
    decay_rate,
    mlp_gain,
    up_weight,
    down_weight,
    link_weight,
    pair_left,
    pair_right,
):
    snaps_here, vertices_here, feature_width = features.shape
    tile_rows = tile_vals.shape[-1]
    slot_count = tile_vals.shape[1]
    per_part = vertices_here // tile_rows
    part_index = lax.axis_index("vert")
    first_block = (part_index - 1) * per_part
    own_first = part_index * per_part
    extended = with_halo(features, (("vert", 1),), vertices_here)
    blocks = extended.reshape(snaps_here, 3 * per_part, tile_rows, feature_width)
    local_src = tile_src - first_block
    local_dst = tile_dst - own_first
    slot_ids = jnp.arange(slot_count, dtype=jnp.int32)[None, :]
    aggregate = tile_terms(blocks, local_src, local_dst, tile_vals, slot_ids < tile_count, per_part)
    combined = aggregate.reshape(snaps_here, vertices_here, feature_width) + features.astype(
        jnp.float32
    )
    normed = root_norm(combined, norm_gain).astype(jnp.bfloat16)
    by_vertex = lax.all_to_all(normed, "snap", split_axis=1, concat_axis=0, tiled=True)
    decays, drives = gate_drive(by_vertex, decay_rate, mix_weight)
    states = run_states(decays, drives, jnp.zeros(decays.shape[1:], jnp.float32))
    vertex_out = feed_forward(states, mlp_gain, up_weight, down_weight)
    embeddings = lax.all_to_all(vertex_out, "snap", split_axis=0, concat_axis=1, tiled=True)
    extended_out = with_halo(embeddings, (("vert", 1),), vertices_here)
    left_side = jnp.einsum(
        "svf,fg->svg", embeddings, link_weight, preferred_element_type=jnp.float32
    ).astype(jnp.bfloat16)
    left_blocks = pick_blocks(
        left_side.reshape(snaps_here, per_part, tile_rows, feature_width), pair_left - own_first
    )
    right_blocks = pick_blocks(
        extended_out.reshape(snaps_here, 3 * per_part, tile_rows, feature_width),
        pair_right - first_block,
    )
    scores = jnp.einsum(
        "spif,spjf->spij", left_blocks, right_blocks, preferred_element_type=jnp.float32
    ) * feature_width ** (-0.5)
    return (embeddings, scores.astype(jnp.bfloat16))


def solution(mesh):
    return jax.shard_map(
        body,
        mesh=mesh,
        in_specs=(
            P("snap", "vert", None),
            P("snap", "vert"),
            P("snap", "vert"),
            P("snap", "vert"),
            P("snap", "vert", None, None),
            P(),
            P(),
            P(),
            P(),
            P(),
            P(),
            P(),
            P("snap", "vert"),
            P("snap", "vert"),
        ),
        out_specs=(P("snap", "vert", None), P("snap", "vert", None, None)),
        check_vma=False,
    )
```

profile of v0, /device:TPU:97, one launch (start us, length us, event | category | flops | bytes accessed | tf_op | source)
XLA Modules:
  0.0 86.9 jit_solution(15219343378757450271)
XLA Ops:
  0.6 0.0 copy-start
  0.6 5.5 %collective-permute-start = (bf16[1,512,256]{2,1,0:T(8,128)(2,1)}, bf16[1,512,256]{2,1,0:T(8,128)(2,1)S(1)}, u32[]{:S(2)}, u32[]{:S(2)}) collective-permute-start(bf16[1,512,256]{2,1,0:T(8,128)(2,1)} %param.18), channel_id=1, source_target_pairs={{0,1},{1,2},{2,3},{3,4},{4,5},{5,6},{6,7},{7,8},{8,9},{9,10},{10,1... | collective-permute-start | bytes 786440 | tf_op jit(solution)/shard_map/ppermute | solution.py:17
  6.1 1.9 %collective-permute-start.1 = (bf16[1,512,256]{2,1,0:T(8,128)(2,1)}, bf16[1,512,256]{2,1,0:T(8,128)(2,1)S(1)}, u32[]{:S(2)}, u32[]{:S(2)}) collective-permute-start(bf16[1,512,256]{2,1,0:T(8,128)(2,1)} %param.18), channel_id=1, source_target_pairs={{1,0},{2,1},{3,2},{4,3},{5,4},{6,5},{7,6},{8,7},{9,8},{10,9},{11,1... | collective-permute-start | bytes 786440 | tf_op jit(solution)/shard_map/ppermute | solution.py:19
  8.0 0.7 and_bitcast_fusion.1
  9.4 0.7 subtract_bitcast_fusion
  10.0 0.7 neg.11
  10.8 0.0 collective-permute-done
  10.8 4.4 %collective-permute-done.1 = bf16[1,512,256]{2,1,0:T(8,128)(2,1)S(1)} collective-permute-done((bf16[1,512,256]{2,1,0:T(8,128)(2,1)}, bf16[1,512,256]{2,1,0:T(8,128)(2,1)S(1)}, u32[]{:S(2)}, u32[]{:S(2)}) %collective-permute-start.1) | collective-permute-done | bytes 262176 | tf_op jit(solution)/shard_map/ppermute | solution.py:19
  15.2 1.0 %pad_maximum_fusion = bf16[1,1536,256]{2,1,0:T(8,128)(2,1)S(1)} fusion(bf16[1,512,256]{2,1,0:T(8,128)(2,1)S(1)} %collective-permute-done.1, bf16[1,512,256]{2,1,0:T(8,128)(2,1)} %param.18, bf16[1,512,256]{2,1,0:T(8,128)(2,1)S(1)} %collective-permute-done), kind=kLoop, calls=%fused_computation.27 | loop fusion | flops 2359296 | bytes 1572864 | tf_op jit(solution)/shard_map/concatenate | solution.py:15
  16.2 2.0 %gather_fusion.1 = bf16[32,128,256]{2,1,0:T(8,128)(2,1)} fusion(bf16[1,12,128,256]{3,2,1,0:T(8,128)(2,1)S(1)} %bitcast.104, s32[32]{0:T(128)S(1)} %or_bitcast_fusion.1), kind=kCustom, calls=%fused_computation.clone | custom fusion | bytes 4194560 | tf_op jit(solution)/shard_map/vmap(jit(_take))/gather | solution.py:35
  18.2 0.0 copy-done
  18.2 4.4 %convolution_bitcast_fusion = f32[32,128,256]{1,2,0:T(8,128)} fusion(bf16[32,128,256]{2,1,0:T(8,128)(2,1)} %gather_fusion.1, pred[32]{0:T(512)(128)(4,1)S(1)} %get-tuple-element.67, bf16[1,32,128,128]{3,2,1,0:T(8,128)(2,1)S(1)} %copy-done), kind=kOutput, calls=%fused_computation.6 | convolution fusion | flops 269484032 | bytes 7340064 | tf_op jit(solution)/shard_map/sgij,sgjf->sgif/dot_general | solution.py:42
  22.6 5.5 %copy.21 = f32[32,128,256]{2,0,1:T(8,128)} copy(f32[32,128,256]{1,2,0:T(8,128)} %convolution_bitcast_fusion) | data formatting | bytes 8388608 | tf_op jit(solution)/shard_map/sgij,sgjf->sgif/dot_general | solution.py:42
  28.1 0.0 copy-start.1
  28.1 0.0 copy-start.4
  28.1 3.7 %fusion.38 = f32[4,128,256]{2,0,1:T(4,128)S(1)} fusion(f32[32,128,256]{2,0,1:T(8,128)} %copy.21, s32[32]{0:T(128)S(1)} %subtract_bitcast_fusion, pred[32]{0:T(512)(128)(4,1)S(1)} %iota_compare_fusion.1), kind=kOutput, calls=%fused_computation.55 | convolution fusion | flops 50331904 | bytes 4718752 | tf_op jit(solution)/shard_map/sgb,sgif->sbif/dot_general | solution.py:45
  31.8 0.1 copy.22
  31.9 0.0 copy-done.1
  31.9 0.0 copy-start.5
  31.9 0.0 copy-start.6
  31.9 0.2 multiply_reduce_fusion.1
  32.1 0.0 copy-done.4
  32.1 0.1 multiply_convert_fusion.5
  32.2 0.0 copy-start.2
  32.3 0.4 copy.27
  32.7 0.5 broadcast.170
  33.2 2.2 %reduce.1 = bf16[512,256]{1,0:T(8,128)(2,1)S(1)} reduce(bf16[512,1,256]{2,1,0:T(2,128)(2,1)S(1)} %bitcast.114, bf16[]{:T(256)} %broadcast.170), dimensions={1}, to_apply=%bitcast.97.reduce_sub_computation | reduce | bytes 524290
  35.4 0.8 reshape.205
  36.2 6.8 %all-to-all-start = ((bf16[16,2,4096]{2,1,0:T(2,128)(2,1)}), bf16[16,2,4096]{2,1,0:T(2,128)(2,1)S(1)}, u32[]{:S(2)}, u32[]{:S(2)}) async-start(bf16[16,2,4096]{2,1,0:T(2,128)(2,1)} %reshape.205), calls=%async_computation | async-start | bytes 524288 | tf_op jit(solution)/shard_map/all_to_all | solution.py:108
  42.9 0.0 copy-done.5
  42.9 0.0 copy-done.6
  43.0 7.3 %all-to-all-done = bf16[16,2,4096]{2,1,0:T(2,128)(2,1)S(1)} async-done(((bf16[16,2,4096]{2,1,0:T(2,128)(2,1)}), bf16[16,2,4096]{2,1,0:T(2,128)(2,1)S(1)}, u32[]{:S(2)}, u32[]{:S(2)}) %all-to-all-start) | async-done | bytes 262176 | tf_op jit(solution)/shard_map/all_to_all | solution.py:108
  50.3 0.3 reshape.206
  50.6 0.0 copy-done.2
  50.6 0.3 fusion.30
  50.9 0.0 copy-start.7
  50.9 0.2 slice_multiply_fusion
  51.1 0.6 while.13
  51.8 0.1 multiply_reduce_fusion
  51.9 0.0 copy-done.7
  52.0 0.0 copy-start.3
  52.0 2.8 %fusion.16 = bf16[16,32,256]{2,1,0:T(8,128)(2,1)} fusion(f32[16,32,256]{2,1,0:T(8,128)S(1)} %get-tuple-element.30, bf16[1024,256]{1,0:T(8,128)(2,1)} %param.28, bf16[256,1024]{1,0:T(8,128)(2,1)} %param.27, f32[256]{0:T(256)S(1)} %copy-done.7, f32[16,32]{1,0:T(8,128)S(1)} %add_rsqrt_fusion), kind=kOutput, calls=%fused_computation.20 | convolution fusion | flops 540147712 | bytes 1838080 | tf_op jit(solution)/shard_map/tnh,hf->tnf/dot_general | solution.py:71
  54.8 3.5 %all-to-all-start.1 = ((bf16[16,32,256]{2,1,0:T(8,128)(2,1)}), bf16[16,32,256]{2,1,0:T(8,128)(2,1)S(1)}, u32[]{:S(2)}, u32[]{:S(2)}) async-start(bf16[16,32,256]{2,1,0:T(8,128)(2,1)} %fusion.16), calls=%async_computation.1 | async-start | bytes 524288 | tf_op jit(solution)/shard_map/all_to_all | solution.py:112
  58.4 7.3 %all-to-all-done.1 = bf16[16,32,256]{2,1,0:T(8,128)(2,1)S(1)} async-done(((bf16[16,32,256]{2,1,0:T(8,128)(2,1)}), bf16[16,32,256]{2,1,0:T(8,128)(2,1)S(1)}, u32[]{:S(2)}, u32[]{:S(2)}) %all-to-all-start.1) | async-done | bytes 262176 | tf_op jit(solution)/shard_map/all_to_all | solution.py:112
  65.6 5.6 %collective-permute-start.2 = (bf16[1,512,256]{2,1,0:T(8,128)(2,1)S(1)}, bf16[1,512,256]{2,1,0:T(8,128)(2,1)S(1)}, u32[]{:S(2)}, u32[]{:S(2)}) collective-permute-start(bf16[1,512,256]{2,1,0:T(8,128)(2,1)S(1)} %bitcast.108), channel_id=1, source_target_pairs={{0,1},{1,2},{2,3},{3,4},{4,5},{5,6},{6,7},{7,8},{8,9},{9,10},{10,1... | collective-permute-start | bytes 786440 | tf_op jit(solution)/shard_map/ppermute | solution.py:17
  71.3 1.9 %collective-permute-start.3 = (bf16[1,512,256]{2,1,0:T(8,128)(2,1)S(1)}, bf16[1,512,256]{2,1,0:T(8,128)(2,1)S(1)}, u32[]{:S(2)}, u32[]{:S(2)}) collective-permute-start(bf16[1,512,256]{2,1,0:T(8,128)(2,1)S(1)} %bitcast.109), channel_id=1, source_target_pairs={{1,0},{2,1},{3,2},{4,3},{5,4},{6,5},{7,6},{8,7},{9,8},{10,9},{11,1... | collective-permute-start | bytes 786440 | tf_op jit(solution)/shard_map/ppermute | solution.py:19
  73.2 0.0 copy-done.3
  73.2 0.2 convolution_convert_fusion
  73.5 2.0 %gather_fusion = bf16[32,128,256]{2,1,0:T(8,128)(2,1)} fusion(bf16[1,4,128,256]{3,2,1,0:T(8,128)(2,1)S(1)} %bitcast.103, s32[32]{0:T(128)S(1)} %or_bitcast_fusion.2), kind=kCustom, calls=%fused_computation.2 | custom fusion | bytes 4194560 | tf_op jit(solution)/shard_map/vmap(jit(_take))/gather | solution.py:35
  75.5 0.0 collective-permute-done.2
  75.5 4.7 %collective-permute-done.3 = bf16[1,512,256]{2,1,0:T(8,128)(2,1)S(1)} collective-permute-done((bf16[1,512,256]{2,1,0:T(8,128)(2,1)S(1)}, bf16[1,512,256]{2,1,0:T(8,128)(2,1)S(1)}, u32[]{:S(2)}, u32[]{:S(2)}) %collective-permute-start.3) | collective-permute-done | bytes 262176 | tf_op jit(solution)/shard_map/ppermute | solution.py:19
  80.2 0.1 pad_maximum_fusion.1
  80.2 2.0 %gather_fusion.2 = bf16[32,128,256]{2,1,0:T(8,128)(2,1)} fusion(bf16[1,12,128,256]{3,2,1,0:T(8,128)(2,1)S(1)} %bitcast.105, s32[32]{0:T(128)S(1)} %or_bitcast_fusion), kind=kCustom, calls=%fused_computation.1.clone | custom fusion | bytes 4194560 | tf_op jit(solution)/shard_map/vmap(jit(_take))/gather | solution.py:35
  82.2 4.0 %fusion.11 = bf16[1,32,128,128]{3,2,1,0:T(8,128)(2,1)} fusion(bf16[32,128,256]{2,1,0:T(8,128)(2,1)} %gather_fusion.2, pred[32]{0:T(512)(128)(4,1)S(1)} %get-tuple-element.63, bf16[32,128,256]{2,1,0:T(8,128)(2,1)} %gather_fusion, pred[32]{0:T(512)(128)(4,1)S(1)} %get-tuple-element.69), kind=kOutput, calls=%fused_computation.18 | convolution fusion | flops 271581184 | bytes 5242944 | tf_op jit(solution)/shard_map/spif,spjf->spij/dot_general | solution.py:124
  86.2 0.7 copy.40
  (29 shorter events, 0.4 us)
Async XLA Ops:
  0.6 17.6 %copy-start = (bf16[1,32,128,128]{3,2,1,0:T(8,128)(2,1)S(1)}, bf16[1,32,128,128]{3,2,1,0:T(8,128)(2,1)}, u32[]{:S(2)}) copy-start(bf16[1,32,128,128]{3,2,1,0:T(8,128)(2,1)} %param.22) | copy-start | bytes 3145732
  0.6 10.1 %collective-permute-start = (bf16[1,512,256]{2,1,0:T(8,128)(2,1)}, bf16[1,512,256]{2,1,0:T(8,128)(2,1)S(1)}, u32[]{:S(2)}, u32[]{:S(2)}) collective-permute-start(bf16[1,512,256]{2,1,0:T(8,128)(2,1)} %param.18), channel_id=1, source_target_pairs={{0,1},{1,2},{2,3},{3,4},{4,5},{5,6},{6,7},{7,8},{8,9},{9,10},{10,1... | collective-permute-start | bytes 786440 | tf_op jit(solution)/shard_map/ppermute | solution.py:17
  6.1 9.1 %collective-permute-start.1 = (bf16[1,512,256]{2,1,0:T(8,128)(2,1)}, bf16[1,512,256]{2,1,0:T(8,128)(2,1)S(1)}, u32[]{:S(2)}, u32[]{:S(2)}) collective-permute-start(bf16[1,512,256]{2,1,0:T(8,128)(2,1)} %param.18), channel_id=1, source_target_pairs={{1,0},{2,1},{3,2},{4,3},{5,4},{6,5},{7,6},{8,7},{9,8},{10,9},{11,1... | collective-permute-start | bytes 786440 | tf_op jit(solution)/shard_map/ppermute | solution.py:19
  28.1 3.8 %copy-start.1 = (bf16[1,512,256]{2,1,0:T(8,128)(2,1)S(1)}, bf16[1,512,256]{2,1,0:T(8,128)(2,1)}, u32[]{:S(2)}) copy-start(bf16[1,512,256]{2,1,0:T(8,128)(2,1)} %param.18) | copy-start | bytes 786436
  28.1 4.0 %copy-start.4 = (f32[256]{0:T(256)S(1)}, f32[256]{0:T(256)}, u32[]{:S(2)}) copy-start(f32[256]{0:T(256)} %param.23) | copy-start | bytes 3076
  31.9 11.1 %copy-start.5 = (s32[1,32]{1,0:T(1,128)S(1)}, s32[1,32]{1,0:T(1,128)}, u32[]{:S(2)}) copy-start(s32[1,32]{1,0:T(1,128)} %param.31) | copy-start | bytes 388
  31.9 11.1 %copy-start.6 = (s32[1,32]{1,0:T(1,128)S(1)}, s32[1,32]{1,0:T(1,128)}, u32[]{:S(2)}) copy-start(s32[1,32]{1,0:T(1,128)} %param.30) | copy-start | bytes 388
  32.2 18.3 %copy-start.2 = (bf16[256,512]{1,0:T(8,128)(2,1)S(1)}, bf16[256,512]{1,0:T(8,128)(2,1)}, u32[]{:S(2)}) copy-start(bf16[256,512]{1,0:T(8,128)(2,1)} %param.24) | copy-start | bytes 786436
  36.2 14.1 %all-to-all-start = ((bf16[16,2,4096]{2,1,0:T(2,128)(2,1)}), bf16[16,2,4096]{2,1,0:T(2,128)(2,1)S(1)}, u32[]{:S(2)}, u32[]{:S(2)}) async-start(bf16[16,2,4096]{2,1,0:T(2,128)(2,1)} %reshape.205), calls=%async_computation | async-start | bytes 524288 | tf_op jit(solution)/shard_map/all_to_all | solution.py:108
  50.9 1.1 %copy-start.7 = (f32[256]{0:T(256)S(1)}, f32[256]{0:T(256)}, u32[]{:S(2)}) copy-start(f32[256]{0:T(256)} %param.26) | copy-start | bytes 3076
  52.0 21.3 %copy-start.3 = (bf16[256,256]{1,0:T(8,128)(2,1)S(1)}, bf16[256,256]{1,0:T(8,128)(2,1)}, u32[]{:S(2)}) copy-start(bf16[256,256]{1,0:T(8,128)(2,1)} %param.29) | copy-start | bytes 393220
  54.8 10.8 %all-to-all-start.1 = ((bf16[16,32,256]{2,1,0:T(8,128)(2,1)}), bf16[16,32,256]{2,1,0:T(8,128)(2,1)S(1)}, u32[]{:S(2)}, u32[]{:S(2)}) async-start(bf16[16,32,256]{2,1,0:T(8,128)(2,1)} %fusion.16), calls=%async_computation.1 | async-start | bytes 524288 | tf_op jit(solution)/shard_map/all_to_all | solution.py:112
  65.6 9.8 %collective-permute-start.2 = (bf16[1,512,256]{2,1,0:T(8,128)(2,1)S(1)}, bf16[1,512,256]{2,1,0:T(8,128)(2,1)S(1)}, u32[]{:S(2)}, u32[]{:S(2)}) collective-permute-start(bf16[1,512,256]{2,1,0:T(8,128)(2,1)S(1)} %bitcast.108), channel_id=1, source_target_pairs={{0,1},{1,2},{2,3},{3,4},{4,5},{5,6},{6,7},{7,8},{8,9},{9,10},{10,1... | collective-permute-start | bytes 786440 | tf_op jit(solution)/shard_map/ppermute | solution.py:17
  71.3 8.9 %collective-permute-start.3 = (bf16[1,512,256]{2,1,0:T(8,128)(2,1)S(1)}, bf16[1,512,256]{2,1,0:T(8,128)(2,1)S(1)}, u32[]{:S(2)}, u32[]{:S(2)}) collective-permute-start(bf16[1,512,256]{2,1,0:T(8,128)(2,1)S(1)} %bitcast.109), channel_id=1, source_target_pairs={{1,0},{2,1},{3,2},{4,3},{5,4},{6,5},{7,6},{8,7},{9,8},{10,9},{11,1... | collective-permute-start | bytes 786440 | tf_op jit(solution)/shard_map/ppermute | solution.py:19
where the time goes:
time: 87.6 us; the launch traced here: 86.9 us
  starting transfers between devices  25.2 us (29%)
  waiting for transfers between devices  23.7 us (27%)
  matrix products  15.4 us (18%)
  local copies, waits for them, and re-layouts  14.4 us (16%)
  other arithmetic  6.3 us (7%)
  between operations  1.6 us (2%)
    ppermute x2, starting transfers between devices, with_halo(): lax.ppermute(tail, axis, [(i, (i + 1) % count) for i in range(ends)])  11.1 us
    ppermute x2, waiting for transfers between devices, with_halo(): lax.ppermute(head, axis, [((i + 1) % count, i) for i in range(ends)])  9.16 us
    all_to_all x1, waiting for transfers between devices, body(): lax.all_to_all(vertex_out, 'snap', split_axis=0, concat_axis=1, tiled=True)  7.28 us
    all_to_all x1, waiting for transfers between devices, body(): lax.all_to_all(normed, 'snap', split_axis=1, concat_axis=0, tiled=True)  7.26 us
    all_to_all x1, starting transfers between devices, body(): lax.all_to_all(normed, 'snap', split_axis=1, concat_axis=0, tiled=True)  6.75 us
    gather x6, local copies, waits for them, and re-layouts, pick_blocks(): jnp.take(source_table, chosen, axis=0)  6.03 us
    dot_general x1, local copies, waits for them, and re-layouts, tile_terms(): jnp.einsum('sgij,sgjf->sgif', tile_part, picked, preferred_element_type=j...  5.47 us
    dot_general x1, matrix products, tile_terms(): jnp.einsum('sgij,sgjf->sgif', tile_part, picked, preferred_element_type=j...  4.37 us
  transfers between devices with their start and end apart: 6, of which 4 were waited for; matrix products, arithmetic and copies ran while one was open for 5% of the time, Pallas kernels for 0%

commit v1 on v0

v1 whole, which is shorter than its diff:
```python
import functools

import jax
import jax.numpy as jnp
from jax import lax
from jax.experimental import pallas as pl
from jax.experimental.pallas import tpu as pltpu
from jax.sharding import PartitionSpec as P

epsilon = 1e-06
VMEM = pl.BlockSpec(memory_space=pltpu.VMEM)
SMEM = pl.BlockSpec(memory_space=pltpu.SMEM)


def call(kernel, outs, in_specs, flops, bytes_accessed, transcendentals=0, scratch=()):
    return pl.pallas_call(
        kernel,
        out_shape=outs,
        in_specs=in_specs,
        out_specs=jax.tree.map(lambda _: VMEM, outs),
        scratch_shapes=list(scratch),
        compiler_params=pltpu.CompilerParams(vmem_limit_bytes=40 * 2**20),
        cost_estimate=pl.CostEstimate(
            flops=flops, bytes_accessed=bytes_accessed, transcendentals=transcendentals
        ),
    )


def block_rows(index, rows):
    return pl.ds(pl.multiple_of(index * rows, rows), rows)


def aggregate_kernel(
    per_part, src, dst, count, own, below, above, tiles, gain, normed, blocks, total
):
    slots, rows, _ = tiles.shape
    vertices = own.shape[0]
    blocks[:vertices] = below[...]
    blocks[vertices : 2 * vertices] = own[...]
    blocks[2 * vertices :] = above[...]
    total[...] = own[...].astype(jnp.float32)
    live = count[0, 0]
    for k in range(slots):
        target = dst[0, k]
        local = lax.rem(target, per_part)
        source = src[0, k] - (target - local) + per_part
        tile = jnp.where(k < live, tiles[k], jnp.zeros((), tiles.dtype))
        total[block_rows(local, rows)] += jnp.dot(
            tile, blocks[block_rows(source, rows)], preferred_element_type=jnp.float32
        )
    combined = total[...]
    scale = lax.rsqrt(jnp.mean(combined * combined, axis=-1, keepdims=True) + epsilon)
    normed[...] = (combined * scale * gain[...]).astype(normed.dtype)


def vertex_kernel(normed, mix, rates, gain, up, down, out):
    steps, rows, width = normed.shape
    state = jnp.zeros((rows, width), jnp.float32)
    group = 4
    for first in range(0, steps, group):
        projected = jnp.dot(
            normed[first : first + group].reshape(group * rows, width),
            mix[...],
            preferred_element_type=jnp.float32,
        )
        gate = 1.0 / (1.0 + jnp.exp(-projected[:, :width]))
        states = []
        for j in range(group):
            part = slice(j * rows, (j + 1) * rows)
            decays = jnp.exp(-rates[first + j : first + j + 1] * gate[part])
            state = decays * state + (1.0 - decays) * projected[part, width:]
            states.append(state)
        states = jnp.concatenate(states)
        scale = lax.rsqrt(jnp.mean(states * states, axis=-1, keepdims=True) + epsilon)
        state_normed = (states * scale * gain[...]).astype(jnp.bfloat16)
        inner = jnp.dot(state_normed, up[...], preferred_element_type=jnp.float32)
        hidden = (inner / (1.0 + jnp.exp(-inner))).astype(jnp.bfloat16)
        result = states + jnp.dot(hidden, down[...], preferred_element_type=jnp.float32)
        out[first : first + group] = result.astype(out.dtype).reshape(group, rows, width)


def left_kernel(embeddings, link, left):
    left[...] = jnp.dot(
        embeddings[...], link[...], preferred_element_type=jnp.float32
    ).astype(left.dtype)


def score_kernel(per_part, pair_left, pair_right, left, own, below, above, scores, blocks):
    pairs, rows, _ = scores.shape
    vertices, width = own.shape
    blocks[:vertices] = below[...]
    blocks[vertices : 2 * vertices] = own[...]
    blocks[2 * vertices :] = above[...]
    for k in range(pairs):
        first = pair_left[0, k]
        local = lax.rem(first, per_part)
        other = pair_right[0, k] - (first - local) + per_part
        product = lax.dot_general(
            left[block_rows(local, rows)],
            blocks[block_rows(other, rows)],
            (((1,), (1,)), ((), ())),
            preferred_element_type=jnp.float32,
        )
        scores[k] = (product * width**-0.5).astype(scores.dtype)


def ring_halo(cells):
    count = lax.axis_size("vert")
    below = lax.ppermute(cells, "vert", [(i, (i + 1) % count) for i in range(count)])
    above = lax.ppermute(cells, "vert", [((i + 1) % count, i) for i in range(count)])
    return below, above


def body(
    features,
    tile_src,
    tile_dst,
    tile_count,
    tile_vals,
    norm_gain,
    mix_weight,
    decay_rate,
    mlp_gain,
    up_weight,
    down_weight,
    link_weight,
    pair_left,
    pair_right,
):
    _, vertices, width = features.shape
    _, slots, rows, _ = tile_vals.shape
    pairs = pair_left.shape[1]
    per_part = vertices // rows
    snaps = lax.axis_size("snap")
    hidden = up_weight.shape[1]
    bf16 = jnp.bfloat16
    own = features.reshape(vertices, width)
    below, above = ring_halo(own)
    normed = call(
        functools.partial(aggregate_kernel, per_part),
        jax.ShapeDtypeStruct((vertices, width), bf16),
        [SMEM, SMEM, SMEM, VMEM, VMEM, VMEM, VMEM, VMEM],
        2 * slots * rows * rows * width,
        2 * slots * rows * rows,
        scratch=[
            pltpu.VMEM((3 * vertices, width), bf16),
            pltpu.VMEM((vertices, width), jnp.float32),
        ],
    )(
        tile_src,
        tile_dst,
        tile_count,
        own,
        below,
        above,
        tile_vals.reshape(slots, rows, rows),
        norm_gain.reshape(1, width),
    )
    by_vertex = lax.all_to_all(
        normed.reshape(snaps, vertices // snaps, width), "snap", 0, 0, tiled=True
    )
    vertex_out = call(
        vertex_kernel,
        jax.ShapeDtypeStruct(by_vertex.shape, bf16),
        [VMEM] * 6,
        2 * vertices * width * (2 * width + 2 * hidden),
        4 * width * (width + hidden),
        vertices * (2 * width + hidden),
    )(
        by_vertex,
        mix_weight,
        decay_rate,
        mlp_gain.reshape(1, width),
        up_weight,
        down_weight,
    )
    embeddings = lax.all_to_all(vertex_out, "snap", 0, 0, tiled=True).reshape(
        vertices, width
    )
    below_out, above_out = ring_halo(embeddings)
    left = call(
        left_kernel,
        jax.ShapeDtypeStruct((vertices, width), bf16),
        [VMEM] * 2,
        2 * vertices * width * width,
        4 * vertices * width,
    )(embeddings, link_weight)
    scores = call(
        functools.partial(score_kernel, per_part),
        jax.ShapeDtypeStruct((pairs, rows, rows), bf16),
        [SMEM, SMEM, VMEM, VMEM, VMEM, VMEM],
        2 * pairs * rows * rows * width,
        2 * pairs * rows * rows,
        scratch=[pltpu.VMEM((3 * vertices, width), bf16)],
    )(pair_left, pair_right, left, embeddings, below_out, above_out)
    return (
        embeddings.reshape(1, vertices, width),
        scores.reshape(1, pairs, rows, rows),
    )


def solution(mesh):
    return jax.shard_map(
        body,
        mesh=mesh,
        in_specs=(
            P("snap", "vert", None),
            P("snap", "vert"),
            P("snap", "vert"),
            P("snap", "vert"),
            P("snap", "vert", None, None),
            P(),
            P(),
            P(),
            P(),
            P(),
            P(),
            P(),
            P("snap", "vert"),
            P("snap", "vert"),
        ),
        out_specs=(P("snap", "vert", None), P("snap", "vert", None, None)),
        check_vma=False,
    )
```

time: 87.6 us -> 58.6 us (0.67)
  the two profiles are of different devices: /device:TPU:97 before, /device:TPU:8 now
where the time goes in v1:
time: 58.6 us; the launch traced here: 58.3 us
  blocking collectives  26.4 us (45%)
  starting transfers between devices  11.9 us (20%)
  waiting for transfers between devices  7.41 us (13%)
  Pallas kernels  6.95 us (12%)
  local copies, waits for them, and re-layouts  4.26 us (7%)
  between operations  1.36 us (2%)
    all_to_all x1, blocking collectives, body(): lax.all_to_all(normed.reshape(snaps, vertices // snaps, width), 'snap', 0...  14.3 us
    all_to_all x1, blocking collectives, body(): lax.all_to_all(vertex_out, 'snap', 0, 0, tiled=True)  12.1 us
    ppermute x2, starting transfers between devices, ring_halo(): lax.ppermute(cells, 'vert', [((i + 1) % count, i) for i in range(count)])  11.9 us
    ppermute x2, waiting for transfers between devices, ring_halo(): lax.ppermute(cells, 'vert', [(i, (i + 1) % count) for i in range(count)])  7.4 us
    unnamed x27, local copies, waits for them, and re-layouts  4.26 us
    pallas_call x1, Pallas kernels, body(): call(functools.partial(aggregate_kernel, per_part), jax.ShapeDtypeStruct(...  2.44 us
    pallas_call x1, Pallas kernels, body(): call(functools.partial(score_kernel, per_part), jax.ShapeDtypeStruct((pai...  2.28 us
    pallas_call x1, Pallas kernels, body(): call(vertex_kernel, jax.ShapeDtypeStruct(by_vertex.shape, bf16), [VMEM] *...  2 us
  transfers between devices with their start and end apart: 4, of which 2 were waited for; matrix products, arithmetic and copies ran while one was open for 0% of the time, Pallas kernels for 0%

profile of v1, /device:TPU:8, one launch (start us, length us, event | category | flops | bytes accessed | tf_op | source)
XLA Modules:
  0.0 58.3 jit_solution(3612824384545649546)
XLA Ops:
  0.6 0.0 collective-permute-start
  0.7 8.9 %collective-permute-start.1 = (bf16[512,256]{1,0:T(8,128)(2,1)}, bf16[512,256]{1,0:T(8,128)(2,1)S(1)}, u32[]{:S(2)}, u32[]{:S(2)}) collective-permute-start(bf16[512,256]{1,0:T(8,128)(2,1)} %bitcast.16), channel_id=1, source_target_pairs={{1,0},{2,1},{3,2},{4,3},{5,4},{6,5},{7,6},{8,7},{9,8},{10,9},{11,1... | collective-permute-start | bytes 786440 | tf_op jit(solution)/shard_map/ppermute | solution.py:110
  10.3 3.6 %collective-permute-done.below = bf16[512,256]{1,0:T(8,128)(2,1)S(1)} collective-permute-done((bf16[512,256]{1,0:T(8,128)(2,1)}, bf16[512,256]{1,0:T(8,128)(2,1)S(1)}, u32[]{:S(2)}, u32[]{:S(2)}) %collective-permute-start) | collective-permute-done | bytes 262176 | tf_op jit(solution)/shard_map/ppermute | solution.py:109
  13.8 0.0 collective-permute-done.1.above
  13.8 0.0 copy-start.5
  13.8 0.0 copy-start.3
  13.9 0.0 copy-start.4
  13.9 0.6 %copy-done.5 = s32[1,32]{1,0:T(1,128)S(1)} copy-done((s32[1,32]{1,0:T(1,128)S(1)}, s32[1,32]{1,0:T(1,128)}, u32[]{:S(2)}) %copy-start.5) | copy-done | bytes 152
  14.5 0.0 copy-done.3
  14.5 0.0 copy-done.4
  14.5 0.0 copy-start
  14.5 1.2 %copy-done = bf16[1,32,128,128]{3,2,1,0:T(8,128)(2,1)S(1)} copy-done((bf16[1,32,128,128]{3,2,1,0:T(8,128)(2,1)S(1)}, bf16[1,32,128,128]{3,2,1,0:T(8,128)(2,1)}, u32[]{:S(2)}) %copy-start) | copy-done | bytes 1048600
  15.8 0.0 copy-start.1
  15.8 0.9 %copy-done.1 = bf16[1,512,256]{2,1,0:T(8,128)(2,1)S(1)} copy-done((bf16[1,512,256]{2,1,0:T(8,128)(2,1)S(1)}, bf16[1,512,256]{2,1,0:T(8,128)(2,1)}, u32[]{:S(2)}) %copy-start.1) | copy-done | bytes 262168
  16.7 0.0 copy-start.9
  16.7 0.0 copy-start.10
  16.7 0.0 copy-start.11
  16.7 2.4 %shard_map.149 = bf16[512,256]{1,0:T(8,128)(2,1)S(1)} custom-call(s32[1,32]{1,0:T(1,128)S(1)} %copy-done.4, s32[1,32]{1,0:T(1,128)S(1)} %copy-done.5, s32[1,1]{1,0:T(1,128)S(6)} %copy.17.count, bf16[512,256]{1,0:T(8,128)(2,1)S(1)} %bitcast.17, bf16[512,256]{1,0:T(8,128)(2,1)S(1)} %collective-permute-done.below, ...), custom_call_target="tpu_custom_call" | custom-call | flops 268435456 | bytes 1048576 | tf_op jit(solution)/shard_map/pallas_call | solution.py:139
  19.2 0.0 copy-start.8
  19.2 14.3 %all_to_all.10.normed = bf16[16,32,256]{2,1,0:T(8,128)(2,1)S(1)} all-to-all(bf16[16,32,256]{2,1,0:T(8,128)(2,1)S(1)} %bitcast.14), channel_id=1, replica_groups=mesh['snap'=16,'vert'=32] {'snap'}, dimensions={0} | all-to-all | bytes 524288 | tf_op jit(solution)/shard_map/all_to_all | solution.py:159
  33.5 0.0 copy-start.12
  33.5 0.0 copy-done.9
  33.5 0.0 copy-done.10
  33.5 0.0 copy-done.11
  33.5 0.0 copy-done.8
  33.5 0.7 %copy-done.12 = f32[256]{0:T(256)S(1)} copy-done((f32[256]{0:T(256)S(1)}, f32[256]{0:T(256)}, u32[]{:S(2)}) %copy-start.12) | copy-done | bytes 1048
  34.2 2.0 %shard_map.150 = bf16[16,32,256]{2,1,0:T(8,128)(2,1)S(1)} custom-call(bf16[16,32,256]{2,1,0:T(8,128)(2,1)S(1)} %all_to_all.10.normed, bf16[256,512]{1,0:T(8,128)(2,1)S(1)} %copy-done.10, f32[16,256]{1,0:T(8,128)S(1)} %copy-done.11, f32[1,256]{1,0:T(1,128)S(1)} %bitcast.19, bf16[256,1024]{1,0:T(8,128)(2,1)S(1)} %copy-done.8, bf16[1024,256]{1,0:T(8,128)(2,1)S(1)} %copy-done.9), custom_call_target="tpu_custom_call" | custom-call | flops 671088640 | bytes 1310720 | tf_op jit(solution)/shard_map/pallas_call | solution.py:162
  36.2 0.0 copy-start.2
  36.2 12.1 %all_to_all.11 = bf16[16,32,256]{2,1,0:T(8,128)(2,1)S(1)} all-to-all(bf16[16,32,256]{2,1,0:T(8,128)(2,1)S(1)} %shard_map.150), channel_id=1, replica_groups=mesh['snap'=16,'vert'=32] {'snap'}, dimensions={0} | all-to-all | bytes 524288 | tf_op jit(solution)/shard_map/all_to_all | solution.py:177
  48.3 0.0 collective-permute-start.2
  48.3 3.0 %collective-permute-start.3 = (bf16[512,256]{1,0:T(8,128)(2,1)S(1)}, bf16[512,256]{1,0:T(8,128)(2,1)S(1)}, u32[]{:S(2)}, u32[]{:S(2)}) collective-permute-start(bf16[512,256]{1,0:T(8,128)(2,1)S(1)} %bitcast.9), channel_id=1, source_target_pairs={{1,0},{2,1},{3,2},{4,3},{5,4},{6,5},{7,6},{8,7},{9,8},{10,9},{11,1... | collective-permute-start | bytes 786440 | tf_op jit(solution)/shard_map/ppermute | solution.py:110
  51.2 0.0 copy-done.2
  51.2 0.0 copy-start.6
  51.2 0.0 copy-start.7
  51.2 0.2 shard_map.151.left
  51.5 3.8 %collective-permute-done.2.below = bf16[512,256]{1,0:T(8,128)(2,1)S(1)} collective-permute-done((bf16[512,256]{1,0:T(8,128)(2,1)S(1)}, bf16[512,256]{1,0:T(8,128)(2,1)S(1)}, u32[]{:S(2)}, u32[]{:S(2)}) %collective-permute-start.2) | collective-permute-done | bytes 262176 | tf_op jit(solution)/shard_map/ppermute | solution.py:109
  55.3 0.0 collective-permute-done.3.above
  55.3 0.0 copy-done.6
  55.3 0.0 copy-done.7
  55.3 2.3 %shard_map.152 = bf16[32,128,128]{2,1,0:T(8,128)(2,1)} custom-call(s32[1,32]{1,0:T(1,128)S(1)} %copy-done.6, s32[1,32]{1,0:T(1,128)S(1)} %copy-done.7, bf16[512,256]{1,0:T(8,128)(2,1)S(1)} %shard_map.151.left, bf16[512,256]{1,0:T(8,128)(2,1)S(1)} %bitcast.11, bf16[512,256]{1,0:T(8,128)(2,1)S(1)} %collective-permute-done.2.below, ...), custom_call_target="tpu_custom_call" | custom-call | flops 268435456 | bytes 1048576 | tf_op jit(solution)/shard_map/pallas_call | solution.py:188
  57.6 0.7 %copy.18 = bf16[1,512,256]{2,1,0:T(8,128)(2,1)} copy(bf16[1,512,256]{2,1,0:T(8,128)(2,1)S(1)} %bitcast.12) | data formatting | bytes 524288
Async XLA Ops:
  0.6 13.2 %collective-permute-start = (bf16[512,256]{1,0:T(8,128)(2,1)}, bf16[512,256]{1,0:T(8,128)(2,1)S(1)}, u32[]{:S(2)}, u32[]{:S(2)}) collective-permute-start(bf16[512,256]{1,0:T(8,128)(2,1)} %bitcast.15), channel_id=1, source_target_pairs={{0,1},{1,2},{2,3},{3,4},{4,5},{5,6},{6,7},{7,8},{8,9},{9,10},{10,1... | collective-permute-start | bytes 786440 | tf_op jit(solution)/shard_map/ppermute | solution.py:109
  0.7 13.2 %collective-permute-start.1 = (bf16[512,256]{1,0:T(8,128)(2,1)}, bf16[512,256]{1,0:T(8,128)(2,1)S(1)}, u32[]{:S(2)}, u32[]{:S(2)}) collective-permute-start(bf16[512,256]{1,0:T(8,128)(2,1)} %bitcast.16), channel_id=1, source_target_pairs={{1,0},{2,1},{3,2},{4,3},{5,4},{6,5},{7,6},{8,7},{9,8},{10,9},{11,1... | collective-permute-start | bytes 786440 | tf_op jit(solution)/shard_map/ppermute | solution.py:110
  13.8 0.7 %copy-start.5 = (s32[1,32]{1,0:T(1,128)S(1)}, s32[1,32]{1,0:T(1,128)}, u32[]{:S(2)}) copy-start(s32[1,32]{1,0:T(1,128)} %dst.1) | copy-start | bytes 388
  13.8 0.7 %copy-start.3 = (f32[256]{0:T(256)S(1)}, f32[256]{0:T(256)}, u32[]{:S(2)}) copy-start(f32[256]{0:T(256)} %param.19) | copy-start | bytes 3076
  13.9 0.7 %copy-start.4 = (s32[1,32]{1,0:T(1,128)S(1)}, s32[1,32]{1,0:T(1,128)}, u32[]{:S(2)}) copy-start(s32[1,32]{1,0:T(1,128)} %src.1) | copy-start | bytes 388
  14.5 1.2 %copy-start = (bf16[1,32,128,128]{3,2,1,0:T(8,128)(2,1)S(1)}, bf16[1,32,128,128]{3,2,1,0:T(8,128)(2,1)}, u32[]{:S(2)}) copy-start(bf16[1,32,128,128]{3,2,1,0:T(8,128)(2,1)} %param.18) | copy-start | bytes 3145732
  15.8 0.9 %copy-start.1 = (bf16[1,512,256]{2,1,0:T(8,128)(2,1)S(1)}, bf16[1,512,256]{2,1,0:T(8,128)(2,1)}, u32[]{:S(2)}) copy-start(bf16[1,512,256]{2,1,0:T(8,128)(2,1)} %param.14) | copy-start | bytes 786436
  16.7 16.8 %copy-start.9 = (bf16[1024,256]{1,0:T(8,128)(2,1)S(1)}, bf16[1024,256]{1,0:T(8,128)(2,1)}, u32[]{:S(2)}) copy-start(bf16[1024,256]{1,0:T(8,128)(2,1)} %down.1) | copy-start | bytes 1572868
  16.7 16.8 %copy-start.10 = (bf16[256,512]{1,0:T(8,128)(2,1)S(1)}, bf16[256,512]{1,0:T(8,128)(2,1)}, u32[]{:S(2)}) copy-start(bf16[256,512]{1,0:T(8,128)(2,1)} %mix.1) | copy-start | bytes 786436
  16.7 16.8 %copy-start.11 = (f32[16,256]{1,0:T(8,128)S(1)}, f32[16,256]{1,0:T(8,128)}, u32[]{:S(2)}) copy-start(f32[16,256]{1,0:T(8,128)} %rates.1) | copy-start | bytes 49156
  19.2 14.3 %copy-start.8 = (bf16[256,1024]{1,0:T(8,128)(2,1)S(1)}, bf16[256,1024]{1,0:T(8,128)(2,1)}, u32[]{:S(2)}) copy-start(bf16[256,1024]{1,0:T(8,128)(2,1)} %up.1) | copy-start | bytes 1572868
  33.5 0.7 %copy-start.12 = (f32[256]{0:T(256)S(1)}, f32[256]{0:T(256)}, u32[]{:S(2)}) copy-start(f32[256]{0:T(256)} %param.22) | copy-start | bytes 3076
  36.2 15.0 %copy-start.2 = (bf16[256,256]{1,0:T(8,128)(2,1)S(1)}, bf16[256,256]{1,0:T(8,128)(2,1)}, u32[]{:S(2)}) copy-start(bf16[256,256]{1,0:T(8,128)(2,1)} %link.1) | copy-start | bytes 393220
  48.3 7.0 %collective-permute-start.2 = (bf16[512,256]{1,0:T(8,128)(2,1)S(1)}, bf16[512,256]{1,0:T(8,128)(2,1)S(1)}, u32[]{:S(2)}, u32[]{:S(2)}) collective-permute-start(bf16[512,256]{1,0:T(8,128)(2,1)S(1)} %bitcast.8), channel_id=1, source_target_pairs={{0,1},{1,2},{2,3},{3,4},{4,5},{5,6},{6,7},{7,8},{8,9},{9,10},{10,1... | collective-permute-start | bytes 786440 | tf_op jit(solution)/shard_map/ppermute | solution.py:109
  48.3 7.0 %collective-permute-start.3 = (bf16[512,256]{1,0:T(8,128)(2,1)S(1)}, bf16[512,256]{1,0:T(8,128)(2,1)S(1)}, u32[]{:S(2)}, u32[]{:S(2)}) collective-permute-start(bf16[512,256]{1,0:T(8,128)(2,1)S(1)} %bitcast.9), channel_id=1, source_target_pairs={{1,0},{2,1},{3,2},{4,3},{5,4},{6,5},{7,6},{8,7},{9,8},{10,9},{11,1... | collective-permute-start | bytes 786440 | tf_op jit(solution)/shard_map/ppermute | solution.py:110
  51.2 4.1 %copy-start.6 = (s32[1,32]{1,0:T(1,128)S(1)}, s32[1,32]{1,0:T(1,128)}, u32[]{:S(2)}) copy-start(s32[1,32]{1,0:T(1,128)} %pair_left.1) | copy-start | bytes 388
  51.2 4.1 %copy-start.7 = (s32[1,32]{1,0:T(1,128)S(1)}, s32[1,32]{1,0:T(1,128)}, u32[]{:S(2)}) copy-start(s32[1,32]{1,0:T(1,128)} %pair_right.1) | copy-start | bytes 388

commit v2 on v1

v2 whole, which is shorter than its diff:
```python
import functools

import jax
import jax.numpy as jnp
from jax import lax
from jax.experimental import pallas as pl
from jax.experimental.pallas import tpu as pltpu
from jax.sharding import PartitionSpec as P

epsilon = 1e-06
VMEM = pl.BlockSpec(memory_space=pltpu.VMEM)
SMEM = pl.BlockSpec(memory_space=pltpu.SMEM)


ANY = pl.BlockSpec(memory_space=pl.ANY)
HBM = pl.BlockSpec(memory_space=pltpu.HBM)


def call(kernel, outs, out_specs, in_specs, cost, scratch=()):
    flops, bytes_accessed, transcendentals = cost
    return pl.pallas_call(
        kernel,
        out_shape=outs,
        in_specs=in_specs,
        out_specs=out_specs,
        scratch_shapes=list(scratch),
        compiler_params=pltpu.CompilerParams(vmem_limit_bytes=40 * 2**20),
        cost_estimate=pl.CostEstimate(
            flops=flops, bytes_accessed=bytes_accessed, transcendentals=transcendentals
        ),
    )


def block_rows(index, rows):
    return pl.ds(pl.multiple_of(index * rows, rows), rows)


def prepare_kernel(
    per_part,
    src,
    dst,
    count,
    pair_left,
    pair_right,
    own,
    tiles,
    norm_gain,
    mlp_gain,
    tile_index,
    pair_index,
    own_out,
    tiles_out,
    norm_gain_out,
    mlp_gain_out,
    sems,
):
    moves = [
        pltpu.make_async_copy(source, target, sems.at[i])
        for i, (source, target) in enumerate(
            (
                (tiles, tiles_out),
                (own, own_out),
                (norm_gain, norm_gain_out),
                (mlp_gain, mlp_gain_out),
            )
        )
    ]
    for move in moves:
        move.start()
    slots = tiles.shape[0]
    for k in range(slots):
        local = lax.rem(dst[0, k], per_part)
        tile_index[0, k] = local
        tile_index[1, k] = src[0, k] - (dst[0, k] - local) + per_part
    for k in range(pair_left.shape[1]):
        local = lax.rem(pair_left[0, k], per_part)
        pair_index[0, k] = local
        pair_index[1, k] = pair_right[0, k] - (pair_left[0, k] - local) + per_part
    for move in moves:
        move.wait()

    @pl.loop(count[0, 0], slots)
    def _(k):
        tiles_out[k] = jnp.zeros_like(tiles_out[k])


def aggregate_kernel(index, own, below, above, tiles, gain, normed, blocks, even, odd):
    slots, rows, _ = tiles.shape
    vertices = own.shape[0]
    blocks[:vertices] = below[...]
    blocks[vertices : 2 * vertices] = own[...]
    blocks[2 * vertices :] = above[...]
    even[...] = own[...].astype(jnp.float32)
    odd[...] = jnp.zeros_like(odd)
    for k in range(slots):
        total = odd if k % 2 else even
        total[block_rows(index[0, k], rows)] += jnp.dot(
            tiles[k],
            blocks[block_rows(index[1, k], rows)],
            preferred_element_type=jnp.float32,
        )
    combined = even[...] + odd[...]
    scale = lax.rsqrt(jnp.mean(combined * combined, axis=-1, keepdims=True) + epsilon)
    normed[...] = (combined * scale * gain[...]).astype(normed.dtype)


def vertex_kernel(normed, mix, rates, gain, up, down, out):
    steps, rows, width = normed.shape
    projected = jnp.dot(
        normed[...].reshape(steps * rows, width),
        mix[...],
        preferred_element_type=jnp.float32,
    )
    gate = 1.0 / (1.0 + jnp.exp(-projected[:, :width]))
    state = jnp.zeros((rows, width), jnp.float32)
    states = []
    for step in range(steps):
        part = slice(step * rows, (step + 1) * rows)
        decays = jnp.exp(-rates[step : step + 1] * gate[part])
        state = decays * state + (1.0 - decays) * projected[part, width:]
        states.append(state)
    states = jnp.concatenate(states)
    scale = lax.rsqrt(jnp.mean(states * states, axis=-1, keepdims=True) + epsilon)
    state_normed = (states * scale * gain[...]).astype(jnp.bfloat16)
    inner = jnp.dot(state_normed, up[...], preferred_element_type=jnp.float32)
    hidden = (inner / (1.0 + jnp.exp(-inner))).astype(jnp.bfloat16)
    result = states + jnp.dot(hidden, down[...], preferred_element_type=jnp.float32)
    out[...] = result.astype(out.dtype).reshape(steps, rows, width)


def left_kernel(embeddings, link, left, kept, sem):
    keep = pltpu.make_async_copy(embeddings, kept, sem)
    keep.start()
    left[...] = jnp.dot(
        embeddings[...], link[...], preferred_element_type=jnp.float32
    ).astype(left.dtype)
    keep.wait()


def score_kernel(index, left, own, below, above, scores, blocks, tiles, sems):
    pairs, rows, _ = scores.shape
    vertices, width = own.shape
    blocks[:vertices] = below[...]
    blocks[vertices : 2 * vertices] = own[...]
    blocks[2 * vertices :] = above[...]
    batch = pairs // sems.shape[0]
    moves = []
    for k in range(pairs):
        product = lax.dot_general(
            left[block_rows(index[0, k], rows)],
            blocks[block_rows(index[1, k], rows)],
            (((1,), (1,)), ((), ())),
            preferred_element_type=jnp.float32,
        )
        tiles[k] = (product * width**-0.5).astype(tiles.dtype)
        if (k + 1) % batch == 0:
            part = pl.ds(k + 1 - batch, batch)
            moves.append(
                pltpu.make_async_copy(tiles.at[part], scores.at[part], sems.at[k // batch])
            )
            moves[-1].start()
    for move in moves:
        move.wait()


def ring_halo(cells):
    count = lax.axis_size("vert")
    below = lax.ppermute(cells, "vert", [(i, (i + 1) % count) for i in range(count)])
    above = lax.ppermute(cells, "vert", [((i + 1) % count, i) for i in range(count)])
    return below, above


def body(
    features,
    tile_src,
    tile_dst,
    tile_count,
    tile_vals,
    norm_gain,
    mix_weight,
    decay_rate,
    mlp_gain,
    up_weight,
    down_weight,
    link_weight,
    pair_left,
    pair_right,
):
    _, vertices, width = features.shape
    _, slots, rows, _ = tile_vals.shape
    pairs = pair_left.shape[1]
    per_part = vertices // rows
    snaps = lax.axis_size("snap")
    hidden = up_weight.shape[1]
    bf16 = jnp.bfloat16
    f32 = jnp.float32
    shape = jax.ShapeDtypeStruct
    own = features.reshape(vertices, width)
    below, above = ring_halo(own)
    tile_index, pair_index, own_near, tiles, norm_row, mlp_row = call(
        functools.partial(prepare_kernel, per_part),
        (
            shape((2, slots), jnp.int32),
            shape((2, pairs), jnp.int32),
            shape((vertices, width), bf16),
            shape((slots, rows, rows), bf16),
            shape((1, width), f32),
            shape((1, width), f32),
        ),
        (SMEM, SMEM, VMEM, VMEM, VMEM, VMEM),
        [SMEM] * 5 + [HBM] * 4,
        (0, 4 * slots * rows * rows, 0),
        [pltpu.SemaphoreType.DMA((4,))],
    )(
        tile_src,
        tile_dst,
        tile_count,
        pair_left,
        pair_right,
        own,
        tile_vals.reshape(slots, rows, rows),
        norm_gain.reshape(1, width),
        mlp_gain.reshape(1, width),
    )
    normed = call(
        aggregate_kernel,
        shape((vertices, width), bf16),
        VMEM,
        [SMEM] + [VMEM] * 5,
        (2 * slots * rows * rows * width, 2 * slots * rows * rows, 0),
        [
            pltpu.VMEM((3 * vertices, width), bf16),
            pltpu.VMEM((vertices, width), f32),
            pltpu.VMEM((vertices, width), f32),
        ],
    )(tile_index, own_near, below, above, tiles, norm_row)
    by_vertex = lax.all_to_all(
        normed.reshape(snaps, vertices // snaps, width), "snap", 0, 0, tiled=True
    )
    vertex_out = call(
        vertex_kernel,
        shape(by_vertex.shape, bf16),
        VMEM,
        [VMEM] * 6,
        (
            2 * vertices * width * (2 * width + 2 * hidden),
            4 * width * (width + hidden),
            vertices * (2 * width + hidden),
        ),
    )(by_vertex, mix_weight, decay_rate, mlp_row, up_weight, down_weight)
    embeddings = lax.all_to_all(vertex_out, "snap", 0, 0, tiled=True).reshape(
        vertices, width
    )
    below_out, above_out = ring_halo(embeddings)
    left, kept = call(
        left_kernel,
        (shape((vertices, width), bf16), shape((vertices, width), bf16)),
        (VMEM, ANY),
        [VMEM] * 2,
        (2 * vertices * width * width, 8 * vertices * width, 0),
        [pltpu.SemaphoreType.DMA],
    )(embeddings, link_weight)
    scores = call(
        score_kernel,
        shape((pairs, rows, rows), bf16),
        ANY,
        [SMEM] + [VMEM] * 4,
        (2 * pairs * rows * rows * width, 2 * pairs * rows * rows, 0),
        [
            pltpu.VMEM((3 * vertices, width), bf16),
            pltpu.VMEM((pairs, rows, rows), bf16),
            pltpu.SemaphoreType.DMA((8,)),
        ],
    )(pair_index, left, embeddings, below_out, above_out)
    return (
        kept.reshape(1, vertices, width),
        scores.reshape(1, pairs, rows, rows),
    )


def solution(mesh):
    return jax.shard_map(
        body,
        mesh=mesh,
        in_specs=(
            P("snap", "vert", None),
            P("snap", "vert"),
            P("snap", "vert"),
            P("snap", "vert"),
            P("snap", "vert", None, None),
            P(),
            P(),
            P(),
            P(),
            P(),
            P(),
            P(),
            P("snap", "vert"),
            P("snap", "vert"),
        ),
        out_specs=(P("snap", "vert", None), P("snap", "vert", None, None)),
        check_vma=False,
    )
```

time: 58.6 us -> 55.5 us (0.947)
  starting transfers between devices: 11.9 us -> 9.46 us
  local copies, waits for them, and re-layouts: 4.26 us -> 2.89 us
    ppermute x2, starting transfers between devices: 11.9 us -> 8.95 us  [ring_halo(): lax.ppermute(cells, 'vert', [((i + 1) % count, i) for i in range(count)])]
    ppermute x2, waiting for transfers between devices: 0.01 us -> 2.65 us  [ring_halo(): lax.ppermute(cells, 'vert', [((i + 1) % count, i) for i in range(count)])]
    ppermute x2, waiting for transfers between devices: 7.4 us -> 5.07 us  [ring_halo(): lax.ppermute(cells, 'vert', [(i, (i + 1) % count) for i in range(count)])]
    unnamed x27 -> x26, local copies, waits for them, and re-layouts: 4.26 us -> 2.89 us
    pallas_call x4 -> x5, Pallas kernels: 6.95 us -> 7.33 us  [the longest x1 2.04 us: body(): call(score_kernel, shape((pairs, rows, rows), bf16), ANY, [SMEM] + [VMEM]...]
  transfers between devices with their start and end apart: 4 -> 4, of which waited for: 2 -> 3; matrix products, arithmetic and copies ran while one was open for 0% -> 0% of each run, Pallas kernels for 0% -> 4%
where the time goes in v2:
time: 55.5 us; the launch traced here: 55.2 us
  blocking collectives  26.4 us (48%)
  starting transfers between devices  9.46 us (17%)
  waiting for transfers between devices  7.72 us (14%)
  Pallas kernels  7.33 us (13%)
  local copies, waits for them, and re-layouts  2.89 us (5%)
  between operations  1.41 us (3%)
    all_to_all x1, blocking collectives, body(): lax.all_to_all(normed.reshape(snaps, vertices // snaps, width), 'snap', 0...  14.3 us
    all_to_all x1, blocking collectives, body(): lax.all_to_all(vertex_out, 'snap', 0, 0, tiled=True)  12.1 us
    ppermute x2, starting transfers between devices, ring_halo(): lax.ppermute(cells, 'vert', [((i + 1) % count, i) for i in range(count)])  8.95 us
    ppermute x2, waiting for transfers between devices, ring_halo(): lax.ppermute(cells, 'vert', [(i, (i + 1) % count) for i in range(count)])  5.07 us
    unnamed x26, local copies, waits for them, and re-layouts  2.89 us
    ppermute x2, waiting for transfers between devices, ring_halo(): lax.ppermute(cells, 'vert', [((i + 1) % count, i) for i in range(count)])  2.65 us
    pallas_call x1, Pallas kernels, body(): call(score_kernel, shape((pairs, rows, rows), bf16), ANY, [SMEM] + [VMEM]...  2.04 us
    pallas_call x1, Pallas kernels, body(): call(functools.partial(prepare_kernel, per_part), (shape((2, slots), jnp....  1.66 us
  transfers between devices with their start and end apart: 4, of which 3 were waited for; matrix products, arithmetic and copies ran while one was open for 0% of the time, Pallas kernels for 4%

profile of v2, /device:TPU:8, one launch (start us, length us, event | category | flops | bytes accessed | tf_op | source)
XLA Modules:
  0.0 55.2 jit_solution(3762215962040878983)
XLA Ops:
  0.6 8.9 %collective-permute-start.1 = (bf16[512,256]{1,0:T(8,128)(2,1)}, bf16[512,256]{1,0:T(8,128)(2,1)S(1)}, u32[]{:S(2)}, u32[]{:S(2)}) collective-permute-start(bf16[512,256]{1,0:T(8,128)(2,1)} %bitcast.14), channel_id=1, source_target_pairs={{1,0},{2,1},{3,2},{4,3},{5,4},{6,5},{7,6},{8,7},{9,8},{10,9},{11,1... | collective-permute-start | bytes 786440 | tf_op jit(solution)/shard_map/ppermute | solution.py:169
  9.6 0.0 collective-permute-start
  10.2 0.0 copy-start.8
  10.2 0.0 copy-start.4
  10.3 0.0 copy-start.6
  10.3 0.0 copy-start.7
  10.3 0.0 copy-start.3
  10.3 0.0 copy-start.5
  10.3 0.6 %copy-done.8 = s32[1,32]{1,0:T(1,128)S(1)} copy-done((s32[1,32]{1,0:T(1,128)S(1)}, s32[1,32]{1,0:T(1,128)}, u32[]{:S(2)}) %copy-start.8) | copy-done | bytes 152
  10.9 0.0 copy-done.4
  10.9 0.0 copy-done.6
  10.9 0.0 copy-done.7
  10.9 0.0 copy-done.3
  11.0 0.0 copy-done.5
  11.0 0.0 copy-start
  11.0 1.2 %copy-done = bf16[1,32,128,128]{3,2,1,0:T(8,128)(2,1)S(1)} copy-done((bf16[1,32,128,128]{3,2,1,0:T(8,128)(2,1)S(1)}, bf16[1,32,128,128]{3,2,1,0:T(8,128)(2,1)}, u32[]{:S(2)}) %copy-start) | copy-done | bytes 1048600
  12.2 0.0 copy-start.1
  12.2 0.9 %copy-done.1 = bf16[1,512,256]{2,1,0:T(8,128)(2,1)S(1)} copy-done((bf16[1,512,256]{2,1,0:T(8,128)(2,1)S(1)}, bf16[1,512,256]{2,1,0:T(8,128)(2,1)}, u32[]{:S(2)}) %copy-start.1) | copy-done | bytes 262168
  13.2 1.7 %shard_map.149 = (s32[2,32]{1,0:T(2,128)S(1)}, s32[2,32]{1,0:T(2,128)S(1)}, bf16[512,256]{1,0:T(8,128)(2,1)S(1)}, bf16[32,128,128]{2,1,0:T(8,128)(2,1)S(1)}, f32[1,256]{1,0:T(1,128)S(1)}, /*index=5*/f32[1,256]{1,0:T(1,128)S(1)}) custom-call(s32[1,32]{1,0:T(1,128)S(1)} %copy-done.5, s32[1,32]{1,0:T(1,128)S(1)} %copy-done.6, s32[1,1]{1,0:T(1,128)S(6)} %copy.16.count, ...), custom_call_target="tpu_custom_call" | custom-call | bytes 2097152 | tf_op jit(solution)/shard_map/pallas_call | solution.py:200
  14.8 0.0 collective-permute-done.1.above
  14.8 2.0 %collective-permute-done.below = bf16[512,256]{1,0:T(8,128)(2,1)S(1)} collective-permute-done((bf16[512,256]{1,0:T(8,128)(2,1)}, bf16[512,256]{1,0:T(8,128)(2,1)S(1)}, u32[]{:S(2)}, u32[]{:S(2)}) %collective-permute-start) | collective-permute-done | bytes 262176 | tf_op jit(solution)/shard_map/ppermute | solution.py:168
  16.8 0.0 copy-start.10
  16.8 0.0 copy-start.11
  16.8 0.0 copy-start.12
  16.8 1.5 %shard_map.150 = bf16[512,256]{1,0:T(8,128)(2,1)S(1)} custom-call(s32[2,32]{1,0:T(2,128)S(1)} %get-tuple-element.10.index, bf16[512,256]{1,0:T(8,128)(2,1)S(1)} %get-tuple-element.11.own, bf16[512,256]{1,0:T(8,128)(2,1)S(1)} %collective-permute-done.below, bf16[512,256]{1,0:T(8,128)(2,1)S(1)} %collective-permute-done.1.above, ...), custom_call_target="tpu_custom_call" | custom-call | flops 268435456 | bytes 1048576 | tf_op jit(solution)/shard_map/pallas_call | solution.py:225
  18.3 0.0 copy-start.9
  18.3 14.3 %all_to_all.10.normed = bf16[16,32,256]{2,1,0:T(8,128)(2,1)S(1)} all-to-all(bf16[16,32,256]{2,1,0:T(8,128)(2,1)S(1)} %bitcast.12), channel_id=1, replica_groups=mesh['snap'=16,'vert'=32] {'snap'}, dimensions={0} | all-to-all | bytes 524288 | tf_op jit(solution)/shard_map/all_to_all | solution.py:237
  32.6 0.0 copy-done.10
  32.6 0.0 copy-done.11
  32.6 0.0 copy-done.12
  32.6 0.0 copy-done.9
  32.7 1.4 %shard_map.151 = bf16[16,32,256]{2,1,0:T(8,128)(2,1)S(1)} custom-call(bf16[16,32,256]{2,1,0:T(8,128)(2,1)S(1)} %all_to_all.10.normed, bf16[256,512]{1,0:T(8,128)(2,1)S(1)} %copy-done.11, f32[16,256]{1,0:T(8,128)S(1)} %copy-done.12, f32[1,256]{1,0:T(1,128)S(1)} %get-tuple-element.14.gain, bf16[256,1024]{1,0:T(8,128)(2,1)S(1)} %copy-done.9, ...), custom_call_target="tpu_custom_call" | custom-call | flops 671088640 | bytes 1310720 | tf_op jit(solution)/shard_map/pallas_call | solution.py:240
  34.0 0.0 copy-start.2
  34.1 12.1 %all_to_all.11 = bf16[16,32,256]{2,1,0:T(8,128)(2,1)S(1)} all-to-all(bf16[16,32,256]{2,1,0:T(8,128)(2,1)S(1)} %shard_map.151), channel_id=1, replica_groups=mesh['snap'=16,'vert'=32] {'snap'}, dimensions={0} | all-to-all | bytes 524288 | tf_op jit(solution)/shard_map/all_to_all | solution.py:251
  46.1 0.0 collective-permute-start.3
  46.1 0.5 collective-permute-start.2
  46.6 0.0 copy-done.2
  46.6 0.7 %shard_map.152 = (bf16[512,256]{1,0:T(8,128)(2,1)S(1)}, bf16[512,256]{1,0:T(8,128)(2,1)}) custom-call(bf16[512,256]{1,0:T(8,128)(2,1)S(1)} %bitcast.10, bf16[256,256]{1,0:T(8,128)(2,1)S(1)} %copy-done.2), custom_call_target="tpu_custom_call" | custom-call | flops 67108864 | bytes 1048576 | tf_op jit(solution)/shard_map/pallas_call | solution.py:255
  47.4 2.6 %collective-permute-done.3.above = bf16[512,256]{1,0:T(8,128)(2,1)S(1)} collective-permute-done((bf16[512,256]{1,0:T(8,128)(2,1)S(1)}, bf16[512,256]{1,0:T(8,128)(2,1)S(1)}, u32[]{:S(2)}, u32[]{:S(2)}) %collective-permute-start.3) | collective-permute-done | bytes 262176 | tf_op jit(solution)/shard_map/ppermute | solution.py:169
  50.0 3.1 %collective-permute-done.2.below = bf16[512,256]{1,0:T(8,128)(2,1)S(1)} collective-permute-done((bf16[512,256]{1,0:T(8,128)(2,1)S(1)}, bf16[512,256]{1,0:T(8,128)(2,1)S(1)}, u32[]{:S(2)}, u32[]{:S(2)}) %collective-permute-start.2) | collective-permute-done | bytes 262176 | tf_op jit(solution)/shard_map/ppermute | solution.py:168
  53.1 2.0 %shard_map.153 = bf16[32,128,128]{2,1,0:T(8,128)(2,1)} custom-call(s32[2,32]{1,0:T(2,128)S(1)} %get-tuple-element.16.index, bf16[512,256]{1,0:T(8,128)(2,1)S(1)} %get-tuple-element.17.left, bf16[512,256]{1,0:T(8,128)(2,1)S(1)} %bitcast.11, bf16[512,256]{1,0:T(8,128)(2,1)S(1)} %collective-permute-done.2.below, bf16[512,256]{1,0:T(8,128)(2,1)S(1)} %collective-permute-done.3.above), custom_call_target="tpu_custom_call" | custom-call | flops 268435456 | bytes 1048576 | tf_op jit(solution)/shard_map/pallas_call | solution.py:263
Async XLA Ops:
  0.6 14.2 %collective-permute-start.1 = (bf16[512,256]{1,0:T(8,128)(2,1)}, bf16[512,256]{1,0:T(8,128)(2,1)S(1)}, u32[]{:S(2)}, u32[]{:S(2)}) collective-permute-start(bf16[512,256]{1,0:T(8,128)(2,1)} %bitcast.14), channel_id=1, source_target_pairs={{1,0},{2,1},{3,2},{4,3},{5,4},{6,5},{7,6},{8,7},{9,8},{10,9},{11,1... | collective-permute-start | bytes 786440 | tf_op jit(solution)/shard_map/ppermute | solution.py:169
  9.6 7.2 %collective-permute-start = (bf16[512,256]{1,0:T(8,128)(2,1)}, bf16[512,256]{1,0:T(8,128)(2,1)S(1)}, u32[]{:S(2)}, u32[]{:S(2)}) collective-permute-start(bf16[512,256]{1,0:T(8,128)(2,1)} %bitcast.15), channel_id=1, source_target_pairs={{0,1},{1,2},{2,3},{3,4},{4,5},{5,6},{6,7},{7,8},{8,9},{9,10},{10,1... | collective-permute-start | bytes 786440 | tf_op jit(solution)/shard_map/ppermute | solution.py:168
  10.2 0.7 %copy-start.8 = (s32[1,32]{1,0:T(1,128)S(1)}, s32[1,32]{1,0:T(1,128)}, u32[]{:S(2)}) copy-start(s32[1,32]{1,0:T(1,128)} %pair_right.1) | copy-start | bytes 388
  10.2 0.7 %copy-start.4 = (f32[256]{0:T(256)S(1)}, f32[256]{0:T(256)}, u32[]{:S(2)}) copy-start(f32[256]{0:T(256)} %param.22) | copy-start | bytes 3076
  10.3 0.7 %copy-start.6 = (s32[1,32]{1,0:T(1,128)S(1)}, s32[1,32]{1,0:T(1,128)}, u32[]{:S(2)}) copy-start(s32[1,32]{1,0:T(1,128)} %dst.1) | copy-start | bytes 388
  10.3 0.7 %copy-start.7 = (s32[1,32]{1,0:T(1,128)S(1)}, s32[1,32]{1,0:T(1,128)}, u32[]{:S(2)}) copy-start(s32[1,32]{1,0:T(1,128)} %pair_left.1) | copy-start | bytes 388
  10.3 0.7 %copy-start.3 = (f32[256]{0:T(256)S(1)}, f32[256]{0:T(256)}, u32[]{:S(2)}) copy-start(f32[256]{0:T(256)} %param.19) | copy-start | bytes 3076
  10.3 0.7 %copy-start.5 = (s32[1,32]{1,0:T(1,128)S(1)}, s32[1,32]{1,0:T(1,128)}, u32[]{:S(2)}) copy-start(s32[1,32]{1,0:T(1,128)} %src.1) | copy-start | bytes 388
  11.0 1.2 %copy-start = (bf16[1,32,128,128]{3,2,1,0:T(8,128)(2,1)S(1)}, bf16[1,32,128,128]{3,2,1,0:T(8,128)(2,1)}, u32[]{:S(2)}) copy-start(bf16[1,32,128,128]{3,2,1,0:T(8,128)(2,1)} %param.18) | copy-start | bytes 3145732
  12.2 0.9 %copy-start.1 = (bf16[1,512,256]{2,1,0:T(8,128)(2,1)S(1)}, bf16[1,512,256]{2,1,0:T(8,128)(2,1)}, u32[]{:S(2)}) copy-start(bf16[1,512,256]{2,1,0:T(8,128)(2,1)} %param.14) | copy-start | bytes 786436
  16.8 15.8 %copy-start.10 = (bf16[1024,256]{1,0:T(8,128)(2,1)S(1)}, bf16[1024,256]{1,0:T(8,128)(2,1)}, u32[]{:S(2)}) copy-start(bf16[1024,256]{1,0:T(8,128)(2,1)} %down.1) | copy-start | bytes 1572868
  16.8 15.8 %copy-start.11 = (bf16[256,512]{1,0:T(8,128)(2,1)S(1)}, bf16[256,512]{1,0:T(8,128)(2,1)}, u32[]{:S(2)}) copy-start(bf16[256,512]{1,0:T(8,128)(2,1)} %mix.1) | copy-start | bytes 786436
  16.8 15.8 %copy-start.12 = (f32[16,256]{1,0:T(8,128)S(1)}, f32[16,256]{1,0:T(8,128)}, u32[]{:S(2)}) copy-start(f32[16,256]{1,0:T(8,128)} %rates.1) | copy-start | bytes 49156
  18.3 14.3 %copy-start.9 = (bf16[256,1024]{1,0:T(8,128)(2,1)S(1)}, bf16[256,1024]{1,0:T(8,128)(2,1)}, u32[]{:S(2)}) copy-start(bf16[256,1024]{1,0:T(8,128)(2,1)} %up.1) | copy-start | bytes 1572868
  34.0 12.6 %copy-start.2 = (bf16[256,256]{1,0:T(8,128)(2,1)S(1)}, bf16[256,256]{1,0:T(8,128)(2,1)}, u32[]{:S(2)}) copy-start(bf16[256,256]{1,0:T(8,128)(2,1)} %link.1) | copy-start | bytes 393220
  46.1 3.9 %collective-permute-start.3 = (bf16[512,256]{1,0:T(8,128)(2,1)S(1)}, bf16[512,256]{1,0:T(8,128)(2,1)S(1)}, u32[]{:S(2)}, u32[]{:S(2)}) collective-permute-start(bf16[512,256]{1,0:T(8,128)(2,1)S(1)} %bitcast.8), channel_id=1, source_target_pairs={{1,0},{2,1},{3,2},{4,3},{5,4},{6,5},{7,6},{8,7},{9,8},{10,9},{11,1... | collective-permute-start | bytes 786440 | tf_op jit(solution)/shard_map/ppermute | solution.py:169
  46.1 7.0 %collective-permute-start.2 = (bf16[512,256]{1,0:T(8,128)(2,1)S(1)}, bf16[512,256]{1,0:T(8,128)(2,1)S(1)}, u32[]{:S(2)}, u32[]{:S(2)}) collective-permute-start(bf16[512,256]{1,0:T(8,128)(2,1)S(1)} %bitcast.9), channel_id=1, source_target_pairs={{0,1},{1,2},{2,3},{3,4},{4,5},{5,6},{6,7},{7,8},{8,9},{9,10},{10,1... | collective-permute-start | bytes 786440 | tf_op jit(solution)/shard_map/ppermute | solution.py:168

commit v3 on v2

--- a/solution.py
+++ b/solution.py
@@ -35,70 +35,85 @@
     return pl.ds(pl.multiple_of(index * rows, rows), rows)
 
 
+def near(own_block, other_block, per_part):
+    first = own_block - lax.rem(own_block, 2 * per_part)
+    other = lax.rem(other_block - first + 3 * per_part, 3 * per_part)
+    return lax.rem(own_block, per_part), other
+
+
+def add_tile(totals, order, index, tiles, blocks, slot, keep):
+    rows = tiles.shape[1]
+    tile = jnp.where(keep, tiles[slot], jnp.zeros((), tiles.dtype))
+    totals[order % 2][block_rows(index[0, slot], rows)] += jnp.dot(
+        tile,
+        blocks[block_rows(index[1, slot], rows)],
+        preferred_element_type=jnp.float32,
+    )
+
+
 def prepare_kernel(
     per_part,
+    count,
     src,
     dst,
-    count,
     pair_left,
     pair_right,
-    own,
-    tiles,
     norm_gain,
     mlp_gain,
+    tiles,
     tile_index,
     pair_index,
-    own_out,
-    tiles_out,
     norm_gain_out,
     mlp_gain_out,
+    tiles_out,
+    src_near,
+    dst_near,
+    left_near,
+    right_near,
     sems,
 ):
+    lists = (
+        (src, src_near),
+        (dst, dst_near),
+        (pair_left, left_near),
+        (pair_right, right_near),
+    )
+    arrays = (
+        (tiles, tiles_out),
+        (norm_gain, norm_gain_out),
+        (mlp_gain, mlp_gain_out),
+    )
     moves = [
         pltpu.make_async_copy(source, target, sems.at[i])
-        for i, (source, target) in enumerate(
-            (
-                (tiles, tiles_out),
-                (own, own_out),
-                (norm_gain, norm_gain_out),
-                (mlp_gain, mlp_gain_out),
-            )
-        )
+        for i, (source, target) in enumerate(lists + arrays)
     ]
     for move in moves:
         move.start()
-    slots = tiles.shape[0]
+    for move in moves[: len(lists)]:
+        move.wait()
+    for k in range(src.shape[1]):
+        tile_index[0, k], tile_index[1, k] = near(
+            dst_near[0, k], src_near[0, k], per_part
+        )
+    tile_index[2, 0] = count[0, 0]
+    for k in range(pair_left.shape[1]):
+        pair_index[0, k], pair_index[1, k] = near(
+            left_near[0, k], right_near[0, k], per_part
+        )
+    for move in moves[len(lists) :]:
+        move.wait()
+
+
+def aggregate_kernel(core, index, pair, halo, tiles, gain, normed, blocks, even, odd):
+    slots, rows, _ = tiles.shape
+    vertices = halo.shape[0]
+    blocks[: 2 * vertices] = pair[...]
+    blocks[2 * vertices :] = halo[...]
+    even[...] = pair[block_rows(core[0], vertices)].astype(jnp.float32)
+    odd[...] = jnp.zeros_like(odd)
+    live = index[2, 0]
     for k in range(slots):
-        local = lax.rem(dst[0, k], per_part)
-        tile_index[0, k] = local
-        tile_index[1, k] = src[0, k] - (dst[0, k] - local) + per_part
-    for k in range(pair_left.shape[1]):
-        local = lax.rem(pair_left[0, k], per_part)
-        pair_index[0, k] = local
-        pair_index[1, k] = pair_right[0, k] - (pair_left[0, k] - local) + per_part
-    for move in moves:
-        move.wait()
-
-    @pl.loop(count[0, 0], slots)
-    def _(k):
-        tiles_out[k] = jnp.zeros_like(tiles_out[k])
-
-
-def aggregate_kernel(index, own, below, above, tiles, gain, normed, blocks, even, odd):
-    slots, rows, _ = tiles.shape
-    vertices = own.shape[0]
-    blocks[:vertices] = below[...]
-    blocks[vertices : 2 * vertices] = own[...]
-    blocks[2 * vertices :] = above[...]
-    even[...] = own[...].astype(jnp.float32)
-    odd[...] = jnp.zeros_like(odd)
-    for k in range(slots):
-        total = odd if k % 2 else even
-        total[block_rows(index[0, k], rows)] += jnp.dot(
-            tiles[k],
-            blocks[block_rows(index[1, k], rows)],
-            preferred_element_type=jnp.float32,
-        )
+        add_tile((even, odd), k, index, tiles, blocks, k, k < live)
     combined = even[...] + odd[...]
     scale = lax.rsqrt(jnp.mean(combined * combined, axis=-1, keepdims=True) + epsilon)
     normed[...] = (combined * scale * gain[...]).astype(normed.dtype)
@@ -137,12 +152,11 @@
     keep.wait()
 
 
-def score_kernel(index, left, own, below, above, scores, blocks, tiles, sems):
+def score_kernel(index, left, pair, halo, scores, blocks, tiles, sems):
     pairs, rows, _ = scores.shape
-    vertices, width = own.shape
-    blocks[:vertices] = below[...]
-    blocks[vertices : 2 * vertices] = own[...]
-    blocks[2 * vertices :] = above[...]
+    vertices, width = halo.shape
+    blocks[: 2 * vertices] = pair[...]
+    blocks[2 * vertices :] = halo[...]
     batch = pairs // sems.shape[0]
     moves = []
     for k in range(pairs):
@@ -163,11 +177,13 @@
         move.wait()
 
 
-def ring_halo(cells):
+def chip_halo(cells):
     count = lax.axis_size("vert")
-    below = lax.ppermute(cells, "vert", [(i, (i + 1) % count) for i in range(count)])
-    above = lax.ppermute(cells, "vert", [((i + 1) % count, i) for i in range(count)])
-    return below, above
+    links = [(i, i + 1) for i in range(1, count - 1, 2)]
+    halo = lax.ppermute(cells, "vert", links + [(j, i) for i, j in links])
+    chips = [[i, i + 1] for i in range(0, count, 2)]
+    pair = lax.all_gather(cells, "vert", axis_index_groups=chips, tiled=True)
+    return pair, halo
 
 
 def body(
@@ -196,44 +212,54 @@
     f32 = jnp.float32
     shape = jax.ShapeDtypeStruct
     own = features.reshape(vertices, width)
-    below, above = ring_halo(own)
-    tile_index, pair_index, own_near, tiles, norm_row, mlp_row = call(
+    core = lax.rem(lax.axis_index("vert"), 2).astype(jnp.int32).reshape(1)
+    pair, halo = chip_halo(own)
+    tile_index, pair_index, norm_row, mlp_row, tiles = call(
         functools.partial(prepare_kernel, per_part),
         (
-            shape((2, slots), jnp.int32),
+            shape((3, slots), jnp.int32),
             shape((2, pairs), jnp.int32),
-            shape((vertices, width), bf16),
-            shape((slots, rows, rows), bf16),
             shape((1, width), f32),
             shape((1, width), f32),
+            shape((slots, rows, rows), bf16),
         ),
-        (SMEM, SMEM, VMEM, VMEM, VMEM, VMEM),
-        [SMEM] * 5 + [HBM] * 4,
+        (SMEM, SMEM, VMEM, VMEM, VMEM),
+        [SMEM] + [HBM] * 7,
         (0, 4 * slots * rows * rows, 0),
-        [pltpu.SemaphoreType.DMA((4,))],
+        [
+            pltpu.SMEM((1, slots), jnp.int32),
+            pltpu.SMEM((1, slots), jnp.int32),
+            pltpu.SMEM((1, pairs), jnp.int32),
+            pltpu.SMEM((1, pairs), jnp.int32),
+            pltpu.SemaphoreType.DMA((7,)),
+        ],
     )(
-        tile_src,
-        tile_dst,
         tile_count,
-        pair_left,
-        pair_right,
-        own,
-        tile_vals.reshape(slots, rows, rows),
-        norm_gain.reshape(1, width),
-        mlp_gain.reshape(1, width),
+        *[
+            pltpu.with_memory_space_constraint(x, pltpu.HBM)
+            for x in (
+                tile_src,
+                tile_dst,
+                pair_left,
+                pair_right,
+                norm_gain.reshape(1, width),
+                mlp_gain.reshape(1, width),
+                tile_vals.reshape(slots, rows, rows),
+            )
+        ]
     )
     normed = call(
         aggregate_kernel,
         shape((vertices, width), bf16),
         VMEM,
-        [SMEM] + [VMEM] * 5,
+        [SMEM] * 2 + [VMEM] * 4,
         (2 * slots * rows * rows * width, 2 * slots * rows * rows, 0),
         [
             pltpu.VMEM((3 * vertices, width), bf16),
             pltpu.VMEM((vertices, width), f32),
             pltpu.VMEM((vertices, width), f32),
         ],
-    )(tile_index, own_near, below, above, tiles, norm_row)
+    )(core, tile_index, pair, halo, tiles, norm_row)
     by_vertex = lax.all_to_all(
         normed.reshape(snaps, vertices // snaps, width), "snap", 0, 0, tiled=True
     )
@@ -251,7 +277,7 @@
     embeddings = lax.all_to_all(vertex_out, "snap", 0, 0, tiled=True).reshape(
         vertices, width
     )
-    below_out, above_out = ring_halo(embeddings)
+    pair_out, halo_out = chip_halo(embeddings)
     left, kept = call(
         left_kernel,
         (shape((vertices, width), bf16), shape((vertices, width), bf16)),
@@ -264,14 +290,14 @@
         score_kernel,
         shape((pairs, rows, rows), bf16),
         ANY,
-        [SMEM] + [VMEM] * 4,
+        [SMEM] + [VMEM] * 3,
         (2 * pairs * rows * rows * width, 2 * pairs * rows * rows, 0),
         [
             pltpu.VMEM((3 * vertices, width), bf16),
             pltpu.VMEM((pairs, rows, rows), bf16),
             pltpu.SemaphoreType.DMA((8,)),
         ],
-    )(pair_index, left, embeddings, below_out, above_out)
+    )(pair_index, left, pair_out, halo_out)
     return (
         kept.reshape(1, vertices, width),
         scores.reshape(1, pairs, rows, rows),

time: 55.5 us -> 51.9 us (0.935)
  the two profiles are of different devices: /device:TPU:8 before, /device:TPU:225 now
where the time goes in v3:
time: 51.9 us; the launch traced here: 51.7 us
  blocking collectives  29.8 us (57%)
  starting transfers between devices  11.6 us (22%)
  Pallas kernels  7.7 us (15%)
  between operations  1.39 us (3%)
  waiting for transfers between devices  1.12 us (2%)
    all_to_all x1, blocking collectives, body(): lax.all_to_all(normed.reshape(snaps, vertices // snaps, width), 'snap', 0...  14.5 us
    ppermute x2, starting transfers between devices, chip_halo(): halo = lax.ppermute(cells, 'vert', links + [(j, i) for i, j in links])  11.6 us
    all_to_all x1, blocking collectives, body(): lax.all_to_all(vertex_out, 'snap', 0, 0, tiled=True)  11 us
    all_gather x2, blocking collectives, chip_halo(): pair = lax.all_gather(cells, 'vert', axis_index_groups=chips, tiled=True)  4.36 us
    pallas_call x1, Pallas kernels, body(): call(score_kernel, shape((pairs, rows, rows), bf16), ANY, [SMEM] + [VMEM]...  2.04 us
    pallas_call x1, Pallas kernels, body(): call(functools.partial(prepare_kernel, per_part), (shape((3, slots), jnp....  1.97 us
    pallas_call x1, Pallas kernels, body(): call(aggregate_kernel, shape((vertices, width), bf16), VMEM, [SMEM] * 2 +...  1.58 us
    pallas_call x1, Pallas kernels, body(): call(vertex_kernel, shape(by_vertex.shape, bf16), VMEM, [VMEM] * 6, (2 *...  1.38 us
  transfers between devices with their start and end apart: 2, of which 1 were waited for; matrix products, arithmetic and copies ran while one was open for 0% of the time, Pallas kernels for 5%

profile of v3, /device:TPU:225, one launch (start us, length us, event | category | flops | bytes accessed | tf_op | source)
XLA Modules:
  0.0 51.7 jit_solution(6488145902065965968)
XLA Ops:
  0.6 5.3 %collective-permute-start = (bf16[512,256]{1,0:T(8,128)(2,1)}, bf16[512,256]{1,0:T(8,128)(2,1)S(1)}, u32[]{:S(2)}, u32[]{:S(2)}) collective-permute-start(bf16[512,256]{1,0:T(8,128)(2,1)} %bitcast.17), channel_id=1, source_target_pairs={{1,2},{3,4},{5,6},{7,8},{9,10},{11,12},{13,14},{15,16},{17,18},{19... | collective-permute-start | bytes 786440 | tf_op jit(solution)/shard_map/ppermute | solution.py:183
  6.6 0.0 copy-start.5
  6.6 2.0 %shard_map.149 = (s32[3,32]{1,0:T(4,128)S(1)}, s32[2,32]{1,0:T(2,128)S(1)}, f32[1,256]{1,0:T(1,128)S(1)}, f32[1,256]{1,0:T(1,128)S(1)}, bf16[32,128,128]{2,1,0:T(8,128)(2,1)S(1)}) custom-call(s32[1,1]{1,0:T(1,128)S(6)} %copy.16.count, s32[1,32]{1,0:T(1,128)} %src.1, s32[1,32]{1,0:T(1,128)} %dst.1, s32[1,32]{1,0:T(1,128)} %pair_left.1, s32[1,32]{1,0:T(1,128)} %pair_right.1, ...), custom_call_target="tpu_custom_call" | custom-call | bytes 2097152 | tf_op jit(solution)/shard_map/pallas_call | solution.py:217
  8.6 0.0 copy-done.5
  8.6 2.2 %all-gather = bf16[1,1024,256]{2,1,0:T(8,128)(2,1)S(1)} all-gather(bf16[1,512,256]{2,1,0:T(8,128)(2,1)S(1)} %copy-done.5), channel_id=2, replica_groups={{0,1},{2,3},{4,5},{6,7},{8,9},{10,11},{12,13},{14,15},{16,17},{18,19},{..., dimensions={1}, use_global_device_ids=true | all-gather | bytes 786432 | tf_op jit(solution)/shard_map/all_gather | solution.py:185
  10.8 0.0 collective-permute-done.halo
  10.8 0.0 copy-start.2
  10.8 0.0 copy-start.3
  10.8 0.0 copy-start.4
  10.8 1.6 %shard_map.150 = bf16[512,256]{1,0:T(8,128)(2,1)S(1)} custom-call(s32[1]{0:T(128)} %bitcast.core, s32[3,32]{1,0:T(4,128)S(1)} %get-tuple-element.9.index, bf16[1024,256]{1,0:T(8,128)(2,1)S(1)} %bitcast.13, bf16[512,256]{1,0:T(8,128)(2,1)S(1)} %collective-permute-done.halo, bf16[32,128,128]{2,1,0:T(8,128)(2,1)S(1)} %get-tuple-element.10.tiles, ...), custom_call_target="tpu_custom_call" | custom-call | flops 268435456 | bytes 1048576 | tf_op jit(solution)/shard_map/pallas_call | solution.py:251
  12.4 0.0 copy-start.1
  12.4 14.5 %all_to_all.10.normed = bf16[16,32,256]{2,1,0:T(8,128)(2,1)S(1)} all-to-all(bf16[16,32,256]{2,1,0:T(8,128)(2,1)S(1)} %bitcast.14), channel_id=1, replica_groups=mesh['snap'=16,'vert'=32] {'snap'}, dimensions={0} | all-to-all | bytes 524288 | tf_op jit(solution)/shard_map/all_to_all | solution.py:263
  26.9 0.0 copy-done.2
  26.9 0.0 copy-done.3
  26.9 0.0 copy-done.4
  26.9 0.0 copy-done.1
  26.9 1.4 %shard_map.151 = bf16[16,32,256]{2,1,0:T(8,128)(2,1)S(1)} custom-call(bf16[16,32,256]{2,1,0:T(8,128)(2,1)S(1)} %all_to_all.10.normed, bf16[256,512]{1,0:T(8,128)(2,1)S(1)} %copy-done.3, f32[16,256]{1,0:T(8,128)S(1)} %copy-done.4, f32[1,256]{1,0:T(1,128)S(1)} %get-tuple-element.12.gain, bf16[256,1024]{1,0:T(8,128)(2,1)S(1)} %copy-done.1, ...), custom_call_target="tpu_custom_call" | custom-call | flops 671088640 | bytes 1310720 | tf_op jit(solution)/shard_map/pallas_call | solution.py:266
  28.3 0.0 copy-start
  28.3 11.0 %all_to_all.11 = bf16[16,32,256]{2,1,0:T(8,128)(2,1)S(1)} all-to-all(bf16[16,32,256]{2,1,0:T(8,128)(2,1)S(1)} %shard_map.151), channel_id=1, replica_groups=mesh['snap'=16,'vert'=32] {'snap'}, dimensions={0} | all-to-all | bytes 524288 | tf_op jit(solution)/shard_map/all_to_all | solution.py:277
  39.3 6.3 %collective-permute-start.1 = (bf16[512,256]{1,0:T(8,128)(2,1)S(1)}, bf16[512,256]{1,0:T(8,128)(2,1)S(1)}, u32[]{:S(2)}, u32[]{:S(2)}) collective-permute-start(bf16[512,256]{1,0:T(8,128)(2,1)S(1)} %bitcast.10), channel_id=1, source_target_pairs={{1,2},{3,4},{5,6},{7,8},{9,10},{11,12},{13,14},{15,16},{17,18},{19... | collective-permute-start | bytes 786440 | tf_op jit(solution)/shard_map/ppermute | solution.py:183
  45.6 0.0 copy-done
  45.6 0.7 %shard_map.152 = (bf16[512,256]{1,0:T(8,128)(2,1)S(1)}, bf16[512,256]{1,0:T(8,128)(2,1)}) custom-call(bf16[512,256]{1,0:T(8,128)(2,1)S(1)} %bitcast.11, bf16[256,256]{1,0:T(8,128)(2,1)S(1)} %copy-done), custom_call_target="tpu_custom_call" | custom-call | flops 67108864 | bytes 1048576 | tf_op jit(solution)/shard_map/pallas_call | solution.py:281
  46.3 2.2 %all_gather.7.pair = bf16[1024,256]{1,0:T(8,128)(2,1)S(1)} all-gather(bf16[512,256]{1,0:T(8,128)(2,1)S(1)} %bitcast.12), channel_id=1, replica_groups={{0,1},{2,3},{4,5},{6,7},{8,9},{10,11},{12,13},{14,15},{16,17},{18,19},{..., dimensions={0}, use_global_device_ids=true | all-gather | bytes 786432 | tf_op jit(solution)/shard_map/all_gather | solution.py:185
  48.5 1.1 %collective-permute-done.1.halo = bf16[512,256]{1,0:T(8,128)(2,1)S(1)} collective-permute-done((bf16[512,256]{1,0:T(8,128)(2,1)S(1)}, bf16[512,256]{1,0:T(8,128)(2,1)S(1)}, u32[]{:S(2)}, u32[]{:S(2)}) %collective-permute-start.1) | collective-permute-done | bytes 262176 | tf_op jit(solution)/shard_map/ppermute | solution.py:183
  49.6 2.0 %shard_map.153 = bf16[32,128,128]{2,1,0:T(8,128)(2,1)} custom-call(s32[2,32]{1,0:T(2,128)S(1)} %get-tuple-element.14.index, bf16[512,256]{1,0:T(8,128)(2,1)S(1)} %get-tuple-element.15.left, bf16[1024,256]{1,0:T(8,128)(2,1)S(1)} %all_gather.7.pair, bf16[512,256]{1,0:T(8,128)(2,1)S(1)} %collective-permute-done.1.halo), custom_call_target="tpu_custom_call" | custom-call | flops 268435456 | bytes 1048576 | tf_op jit(solution)/shard_map/pallas_call | solution.py:289
Async XLA Ops:
  0.6 10.2 %collective-permute-start = (bf16[512,256]{1,0:T(8,128)(2,1)}, bf16[512,256]{1,0:T(8,128)(2,1)S(1)}, u32[]{:S(2)}, u32[]{:S(2)}) collective-permute-start(bf16[512,256]{1,0:T(8,128)(2,1)} %bitcast.17), channel_id=1, source_target_pairs={{1,2},{3,4},{5,6},{7,8},{9,10},{11,12},{13,14},{15,16},{17,18},{19... | collective-permute-start | bytes 786440 | tf_op jit(solution)/shard_map/ppermute | solution.py:183
  6.6 2.0 %copy-start.5 = (bf16[1,512,256]{2,1,0:T(8,128)(2,1)S(1)}, bf16[1,512,256]{2,1,0:T(8,128)(2,1)}, u32[]{:S(2)}) copy-start(bf16[1,512,256]{2,1,0:T(8,128)(2,1)} %param.14) | copy-start | bytes 786436
  10.8 16.1 %copy-start.2 = (bf16[1024,256]{1,0:T(8,128)(2,1)S(1)}, bf16[1024,256]{1,0:T(8,128)(2,1)}, u32[]{:S(2)}) copy-start(bf16[1024,256]{1,0:T(8,128)(2,1)} %down.1) | copy-start | bytes 1572868
  10.8 16.1 %copy-start.3 = (bf16[256,512]{1,0:T(8,128)(2,1)S(1)}, bf16[256,512]{1,0:T(8,128)(2,1)}, u32[]{:S(2)}) copy-start(bf16[256,512]{1,0:T(8,128)(2,1)} %mix.1) | copy-start | bytes 786436
  10.8 16.1 %copy-start.4 = (f32[16,256]{1,0:T(8,128)S(1)}, f32[16,256]{1,0:T(8,128)}, u32[]{:S(2)}) copy-start(f32[16,256]{1,0:T(8,128)} %rates.1) | copy-start | bytes 49156
  12.4 14.5 %copy-start.1 = (bf16[256,1024]{1,0:T(8,128)(2,1)S(1)}, bf16[256,1024]{1,0:T(8,128)(2,1)}, u32[]{:S(2)}) copy-start(bf16[256,1024]{1,0:T(8,128)(2,1)} %up.1) | copy-start | bytes 1572868
  28.3 17.3 %copy-start = (bf16[256,256]{1,0:T(8,128)(2,1)S(1)}, bf16[256,256]{1,0:T(8,128)(2,1)}, u32[]{:S(2)}) copy-start(bf16[256,256]{1,0:T(8,128)(2,1)} %link.1) | copy-start | bytes 393220
  39.3 10.3 %collective-permute-start.1 = (bf16[512,256]{1,0:T(8,128)(2,1)S(1)}, bf16[512,256]{1,0:T(8,128)(2,1)S(1)}, u32[]{:S(2)}, u32[]{:S(2)}) collective-permute-start(bf16[512,256]{1,0:T(8,128)(2,1)S(1)} %bitcast.10), channel_id=1, source_target_pairs={{1,2},{3,4},{5,6},{7,8},{9,10},{11,12},{13,14},{15,16},{17,18},{19... | collective-permute-start | bytes 786440 | tf_op jit(solution)/shard_map/ppermute | solution.py:183

commit v4 on v2

v4 whole, which is shorter than its diff:
```python
import functools

import jax
import jax.numpy as jnp
from jax import lax
from jax.experimental import pallas as pl
from jax.experimental.pallas import tpu as pltpu
from jax.sharding import PartitionSpec as P

epsilon = 1e-06
list_rows = 16
VMEM = pl.BlockSpec(memory_space=pltpu.VMEM)
SMEM = pl.BlockSpec(memory_space=pltpu.SMEM)


ANY = pl.BlockSpec(memory_space=pl.ANY)
HBM = pl.BlockSpec(memory_space=pltpu.HBM)


def call(kernel, outs, out_specs, in_specs, cost, scratch=()):
    flops, bytes_accessed, transcendentals = cost
    return pl.pallas_call(
        kernel,
        out_shape=outs,
        in_specs=in_specs,
        out_specs=out_specs,
        scratch_shapes=list(scratch),
        compiler_params=pltpu.CompilerParams(vmem_limit_bytes=40 * 2**20),
        cost_estimate=pl.CostEstimate(
            flops=flops, bytes_accessed=bytes_accessed, transcendentals=transcendentals
        ),
    )


def block_rows(index, rows):
    return pl.ds(pl.multiple_of(index * rows, rows), rows)


def near(own_block, other_block, per_part):
    other = other_block - (own_block & -(2 * per_part)) + 3 * per_part
    other = jnp.where(other >= 3 * per_part, other - 3 * per_part, other)
    return own_block & (per_part - 1), other


def core_index():
    return lax.rem(lax.axis_index("vert"), 2)


def prepare_kernel(count, src, dst, own, joined, src_near, dst_near, row, sems):
    vertices, width = own.shape
    slots = src.shape[1]
    lanes = width // 2
    row[...] = jnp.full(row.shape, count[0, 0], jnp.int32)
    moves = [
        pltpu.make_async_copy(source, target, sems.at[i])
        for i, (source, target) in enumerate(
            ((src, src_near), (dst, dst_near), (own, joined.at[:vertices]))
        )
    ]
    for move in moves:
        move.start()
    for move in moves[:2]:
        move.wait()
    row[:, :slots] = src_near[...]
    row[:, lanes : lanes + slots] = dst_near[...]
    trailer = row[...].astype(jnp.float32).astype(joined.dtype)
    joined[vertices:] = jnp.broadcast_to(trailer, (list_rows, width))
    moves[2].wait()


def blocks_kernel(
    per_part, gain, out_gain, pair, halo, blocks, lists, own, gain_near, out_gain_near, sems
):
    vertices, width = halo.shape
    stride = pair.shape[0] // 2
    mate = 1 - core_index()
    loads = [
        pltpu.make_async_copy(gain, gain_near, sems.at[0]),
        pltpu.make_async_copy(out_gain, out_gain_near, sems.at[1]),
    ]
    for load in loads:
        load.start()
    place = pl.multiple_of(mate * stride, list_rows)
    start = pl.multiple_of(mate * stride + vertices, list_rows)
    trailer = pair[pl.ds(start, list_rows)].astype(jnp.float32)[:1].astype(jnp.int32)
    lanes = width // 2
    lists[0:1], lists[1:2] = near(trailer[:, lanes:], trailer[:, :lanes], per_part)
    lists[2:3] = trailer[:, :lanes]
    blocks[:vertices] = pair[:vertices]
    blocks[vertices : 2 * vertices] = pair[stride : stride + vertices]
    blocks[2 * vertices :] = halo[...]
    own[...] = pair[pl.ds(place, vertices)].astype(jnp.float32)
    for load in loads:
        load.wait()


def aggregate_kernel(lists, blocks, own, gain, tiles, normed, even, odd, index, sem):
    slots, rows, _ = tiles.shape
    fetch = pltpu.make_async_copy(lists, index, sem)
    fetch.start()
    even[...] = own[...]
    odd[...] = jnp.zeros_like(odd)
    fetch.wait()
    live = index[2, slots]
    for k in range(slots):
        total = odd if k % 2 else even
        total[block_rows(index[0, k], rows)] += jnp.dot(
            jnp.where(k < live, tiles[k], jnp.zeros((), tiles.dtype)),
            blocks[block_rows(index[1, k], rows)],
            preferred_element_type=jnp.float32,
        )
    combined = even[...] + odd[...]
    scale = lax.rsqrt(jnp.mean(combined * combined, axis=-1, keepdims=True) + epsilon)
    normed[...] = (combined * scale * gain[...]).astype(normed.dtype)


def vertex_kernel(gain, normed, mix, rates, up, down, out):
    steps, rows, width = normed.shape
    projected = jnp.dot(
        normed[...].reshape(steps * rows, width),
        mix[...],
        preferred_element_type=jnp.float32,
    )
    gate = 1.0 / (1.0 + jnp.exp(-projected[:, :width]))
    state = jnp.zeros((rows, width), jnp.float32)
    states = []
    for step in range(steps):
        part = slice(step * rows, (step + 1) * rows)
        decays = jnp.exp(-rates[step : step + 1] * gate[part])
        state = decays * state + (1.0 - decays) * projected[part, width:]
        states.append(state)
    states = jnp.concatenate(states)
    scale = lax.rsqrt(jnp.mean(states * states, axis=-1, keepdims=True) + epsilon)
    state_normed = (states * scale * gain[...]).astype(jnp.bfloat16)
    inner = jnp.dot(state_normed, up[...], preferred_element_type=jnp.float32)
    hidden = (inner / (1.0 + jnp.exp(-inner))).astype(jnp.bfloat16)
    result = states + jnp.dot(hidden, down[...], preferred_element_type=jnp.float32)
    out[...] = result.astype(out.dtype).reshape(steps, rows, width)


def left_kernel(
    per_part, pair_left, pair_right, pair, link, left, kept, lists, left_near, right_near, sems
):
    own = block_rows(1 - core_index(), left.shape[0])
    moves = [
        pltpu.make_async_copy(source, target, sems.at[i])
        for i, (source, target) in enumerate(
            ((pair_left, left_near), (pair_right, right_near), (pair.at[own], kept))
        )
    ]
    for move in moves:
        move.start()
    left[...] = jnp.dot(
        pair[own], link[...], preferred_element_type=jnp.float32
    ).astype(left.dtype)
    for move in moves[:2]:
        move.wait()
    pairs = left_near.shape[1]
    lists[0:1, :pairs], right = near(left_near[...], right_near[...], per_part)
    lists[1:2, :pairs] = jnp.where(right < 2 * per_part, right ^ per_part, right)
    moves[2].wait()


def score_kernel(lists, left, pair, halo, scores, blocks, tiles, index, fetch_sem, sems):
    pairs, rows, _ = scores.shape
    vertices, width = halo.shape
    fetch = pltpu.make_async_copy(lists, index, fetch_sem)
    fetch.start()
    blocks[: 2 * vertices] = pair[...]
    blocks[2 * vertices :] = halo[...]
    fetch.wait()
    batch = pairs // sems.shape[0]
    moves = []
    for k in range(pairs):
        product = lax.dot_general(
            left[block_rows(index[0, k], rows)],
            blocks[block_rows(index[1, k], rows)],
            (((1,), (1,)), ((), ())),
            preferred_element_type=jnp.float32,
        )
        tiles[k] = (product * width**-0.5).astype(tiles.dtype)
        if (k + 1) % batch == 0:
            part = pl.ds(k + 1 - batch, batch)
            moves.append(
                pltpu.make_async_copy(tiles.at[part], scores.at[part], sems.at[k // batch])
            )
            moves[-1].start()
    for move in moves:
        move.wait()


def in_hbm(array):
    return pltpu.with_memory_space_constraint(array, pltpu.HBM)


def zigzag(cells, up):
    count = lax.axis_size("vert")
    order = list(range(0, count, 2)) + list(range(count - 1, 0, -2))
    links = list(zip(order, order[1:] + order[:1]))
    return lax.ppermute(cells, "vert", links if up else [(j, i) for i, j in links])


def chip_pair(cells):
    count = lax.axis_size("vert")
    chips = [[i, i + 1] for i in range(0, count, 2)]
    return lax.all_gather(cells, "vert", axis_index_groups=chips, tiled=True)


def body(
    features,
    tile_src,
    tile_dst,
    tile_count,
    tile_vals,
    norm_gain,
    mix_weight,
    decay_rate,
    mlp_gain,
    up_weight,
    down_weight,
    link_weight,
    pair_left,
    pair_right,
):
    _, vertices, width = features.shape
    _, slots, rows, _ = tile_vals.shape
    pairs = pair_left.shape[1]
    per_part = vertices // rows
    snaps = lax.axis_size("snap")
    hidden = up_weight.shape[1]
    bf16 = jnp.bfloat16
    f32 = jnp.float32
    shape = jax.ShapeDtypeStruct
    own = features.reshape(vertices, width)
    halo = zigzag(own, up=False)
    joined = call(
        prepare_kernel,
        shape((vertices + list_rows, width), bf16),
        VMEM,
        [SMEM] + [HBM] * 3,
        (0, 4 * vertices * width, 0),
        [
            pltpu.VMEM((1, slots), jnp.int32),
            pltpu.VMEM((1, slots), jnp.int32),
            pltpu.VMEM((1, width), jnp.int32),
            pltpu.SemaphoreType.DMA((3,)),
        ],
    )(tile_count, in_hbm(tile_src), in_hbm(tile_dst), in_hbm(own))
    tiles = lax.ppermute(
        tile_vals.reshape(slots, rows, rows),
        "vert",
        [(i, i ^ 1) for i in range(lax.axis_size("vert"))],
    )
    pair = chip_pair(joined)
    blocks, tile_lists, base, gain, out_gain = call(
        functools.partial(blocks_kernel, per_part),
        (
            shape((3 * vertices, width), bf16),
            shape((8, width // 2), jnp.int32),
            shape((vertices, width), f32),
            shape((1, width), f32),
            shape((1, width), f32),
        ),
        (VMEM,) * 5,
        [HBM] * 2 + [VMEM] * 2,
        (2**34, 8 * vertices * width, 0),
        [pltpu.SemaphoreType.DMA((2,))],
    )(
        in_hbm(norm_gain.reshape(1, width)),
        in_hbm(mlp_gain.reshape(1, width)),
        pair,
        halo,
    )
    normed = call(
        aggregate_kernel,
        shape((vertices, width), bf16),
        VMEM,
        [VMEM] * 5,
        (2 * slots * rows * rows * width, 2 * slots * rows * rows, 0),
        [
            pltpu.VMEM((vertices, width), f32),
            pltpu.VMEM((vertices, width), f32),
            pltpu.SMEM((8, width // 2), jnp.int32),
            pltpu.SemaphoreType.DMA,
        ],
    )(tile_lists, blocks, base, gain, tiles)
    by_vertex = lax.all_to_all(
        normed.reshape(snaps, vertices // snaps, width), "snap", 0, 0, tiled=True
    )
    vertex_out = call(
        vertex_kernel,
        shape(by_vertex.shape, bf16),
        VMEM,
        [VMEM] * 6,
        (
            2 * vertices * width * (2 * width + 2 * hidden),
            4 * width * (width + hidden),
            vertices * (2 * width + hidden),
        ),
    )(
        out_gain,
        by_vertex,
        mix_weight,
        decay_rate,
        up_weight,
        down_weight,
    )
    embeddings = lax.all_to_all(vertex_out, "snap", 0, 0, tiled=True).reshape(
        vertices, width
    )
    halo_out = zigzag(embeddings, up=True)
    pair_out = chip_pair(embeddings)
    left, kept, lists = call(
        functools.partial(left_kernel, per_part),
        (
            shape((vertices, width), bf16),
            shape((vertices, width), bf16),
            shape((8, width // 2), jnp.int32),
        ),
        (VMEM, ANY, VMEM),
        [HBM] * 2 + [VMEM] * 2,
        (2 * vertices * width * width, 8 * vertices * width, 0),
        [
            pltpu.VMEM((1, pairs), jnp.int32),
            pltpu.VMEM((1, pairs), jnp.int32),
            pltpu.SemaphoreType.DMA((3,)),
        ],
    )(in_hbm(pair_left), in_hbm(pair_right), pair_out, link_weight)
    scores = call(
        score_kernel,
        shape((pairs, rows, rows), bf16),
        ANY,
        [VMEM] * 4,
        (2 * pairs * rows * rows * width, 2 * pairs * rows * rows, 0),
        [
            pltpu.VMEM((3 * vertices, width), bf16),
            pltpu.VMEM((pairs, rows, rows), bf16),
            pltpu.SMEM((8, width // 2), jnp.int32),
            pltpu.SemaphoreType.DMA,
            pltpu.SemaphoreType.DMA((8,)),
        ],
    )(lists, left, pair_out, halo_out)
    return (
        kept.reshape(1, vertices, width),
        scores.reshape(1, pairs, rows, rows),
    )


def solution(mesh):
    return jax.shard_map(
        body,
        mesh=mesh,
        in_specs=(
            P("snap", "vert", None),
            P("snap", "vert"),
            P("snap", "vert"),
            P("snap", "vert"),
            P("snap", "vert", None, None),
            P(),
            P(),
            P(),
            P(),
            P(),
            P(),
            P(),
            P("snap", "vert"),
            P("snap", "vert"),
        ),
        out_specs=(P("snap", "vert", None), P("snap", "vert", None, None)),
        check_vma=False,
    )
```

time: 55.5 us -> 50.4 us (0.908)
  the two profiles are of different devices: /device:TPU:8 before, /device:TPU:384 now
where the time goes in v4:
time: 50.4 us; the launch traced here: 50.1 us
  blocking collectives  32.6 us (65%)
  Pallas kernels  7.44 us (15%)
  waiting for transfers between devices  4.52 us (9%)
  starting transfers between devices  4.14 us (8%)
  between operations  1.38 us (3%)
    all_to_all x1, blocking collectives, body(): lax.all_to_all(normed.reshape(snaps, vertices // snaps, width), 'snap', 0...  16 us
    all_to_all x1, blocking collectives, body(): lax.all_to_all(vertex_out, 'snap', 0, 0, tiled=True)  11.9 us
    all_gather x2, blocking collectives, chip_pair(): return lax.all_gather(cells, 'vert', axis_index_groups=chips, tiled=True)  4.62 us
    ppermute x2, waiting for transfers between devices, zigzag(): lax.ppermute(cells, 'vert', links if up else [(j, i) for i, j in links])  4.52 us
    ppermute x2, starting transfers between devices, zigzag(): lax.ppermute(cells, 'vert', links if up else [(j, i) for i, j in links])  2.24 us
    pallas_call x1, Pallas kernels, body(): call(score_kernel, shape((pairs, rows, rows), bf16), ANY, [VMEM] * 4, (2...  2.05 us
    ppermute x1, starting transfers between devices, body(): lax.ppermute(tile_vals.reshape(slots, rows, rows), 'vert', [(i, i ^ 1) fo...  1.91 us
    pallas_call x1, Pallas kernels, body(): call(aggregate_kernel, shape((vertices, width), bf16), VMEM, [VMEM] * 5,...  1.55 us
  transfers between devices with their start and end apart: 3, of which 1 were waited for; matrix products, arithmetic and copies ran while one was open for 0% of the time, Pallas kernels for 5%

profile of v4, /device:TPU:384, one launch (start us, length us, event | category | flops | bytes accessed | tf_op | source)
XLA Modules:
  0.0 50.1 jit_solution(9915806121262409404)
XLA Ops:
  0.6 2.2 %collective-permute-start = (bf16[512,256]{1,0:T(8,128)(2,1)}, bf16[512,256]{1,0:T(8,128)(2,1)S(1)}, u32[]{:S(2)}, u32[]{:S(2)}) collective-permute-start(bf16[512,256]{1,0:T(8,128)(2,1)} %bitcast.12), channel_id=1, source_target_pairs={{2,0},{4,2},{6,4},{8,6},{10,8},{12,10},{14,12},{16,14},{18,16},{20... | collective-permute-start | bytes 786440 | tf_op jit(solution)/shard_map/ppermute | solution.py:200
  2.9 1.9 %collective-permute-start.1 = (bf16[32,128,128]{2,1,0:T(8,128)(2,1)}, bf16[32,128,128]{2,1,0:T(8,128)(2,1)S(1)}, u32[]{:S(2)}, u32[]{:S(2)}) collective-permute-start(bf16[32,128,128]{2,1,0:T(8,128)(2,1)} %bitcast.14), channel_id=1, source_target_pairs={{0,1},{1,0},{2,3},{3,2},{4,5},{5,4},{6,7},{7,6},{8,9},{9,8},{10,11... | collective-permute-start | bytes 3145736 | tf_op jit(solution)/shard_map/ppermute | solution.py:249
  5.4 1.0 %shard_map.149 = bf16[528,256]{1,0:T(8,128)(2,1)S(1)} custom-call(s32[1,1]{1,0:T(1,128)S(6)} %copy.16.count, s32[1,32]{1,0:T(1,128)} %src.1, s32[1,32]{1,0:T(1,128)} %dst.1, bf16[512,256]{1,0:T(8,128)(2,1)} %bitcast.13), custom_call_target="tpu_custom_call" | custom-call | bytes 524288 | tf_op jit(solution)/shard_map/pallas_call | solution.py:236
  6.4 2.3 %all_gather.6.pair = bf16[1056,256]{1,0:T(8,128)(2,1)S(1)} all-gather(bf16[528,256]{1,0:T(8,128)(2,1)S(1)} %shard_map.149), channel_id=1, replica_groups={{0,1},{2,3},{4,5},{6,7},{8,9},{10,11},{12,13},{14,15},{16,17},{18,19},{..., dimensions={0}, use_global_device_ids=true | all-gather | bytes 811008 | tf_op jit(solution)/shard_map/all_gather | solution.py:206
  8.8 0.0 collective-permute-done.halo
  8.8 0.7 %shard_map.150 = (bf16[1536,256]{1,0:T(8,128)(2,1)S(1)}, s32[8,128]{1,0:T(8,128)S(1)}, f32[512,256]{1,0:T(8,128)S(1)}, f32[1,256]{1,0:T(1,128)S(1)}, f32[1,256]{1,0:T(1,128)S(1)}) custom-call(f32[1,256]{1,0:T(1,128)} %bitcast.16, f32[1,256]{1,0:T(1,128)} %bitcast.17, bf16[1056,256]{1,0:T(8,128)(2,1)S(1)} %all_gather.6.pair, ...), custom_call_target="tpu_custom_call" | custom-call | flops 17179869184 | bytes 1048576 | tf_op jit(solution)/shard_map/pallas_call | solution.py:255
  9.5 0.0 collective-permute-done.1.tiles
  9.5 0.0 copy-start.2
  9.5 0.0 copy-start.3
  9.5 0.0 copy-start.4
  9.5 1.5 %shard_map.151 = bf16[512,256]{1,0:T(8,128)(2,1)S(1)} custom-call(s32[8,128]{1,0:T(8,128)S(1)} %get-tuple-element.11.lists, bf16[1536,256]{1,0:T(8,128)(2,1)S(1)} %get-tuple-element.12.blocks, f32[512,256]{1,0:T(8,128)S(1)} %get-tuple-element.13.own, f32[1,256]{1,0:T(1,128)S(1)} %get-tuple-element.14.gain, bf16[32,128,128]{2,1,0:T(8,128)(2,1)S(1)} %collective-permute-done.1.tiles), custom_call_target="tpu_custom_call" | custom-call | flops 268435456 | bytes 1048576 | tf_op jit(solution)/shard_map/pallas_call | solution.py:274
  11.1 0.0 copy-start.1
  11.1 16.0 %all_to_all.10.normed = bf16[16,32,256]{2,1,0:T(8,128)(2,1)S(1)} all-to-all(bf16[16,32,256]{2,1,0:T(8,128)(2,1)S(1)} %bitcast.8), channel_id=1, replica_groups=mesh['snap'=16,'vert'=32] {'snap'}, dimensions={0} | all-to-all | bytes 524288 | tf_op jit(solution)/shard_map/all_to_all | solution.py:287
  27.1 0.0 copy-done.2
  27.1 0.0 copy-done.3
  27.1 0.0 copy-done.4
  27.1 0.0 copy-done.1
  27.1 1.4 %shard_map.152 = bf16[16,32,256]{2,1,0:T(8,128)(2,1)S(1)} custom-call(f32[1,256]{1,0:T(1,128)S(1)} %get-tuple-element.10.gain, bf16[16,32,256]{2,1,0:T(8,128)(2,1)S(1)} %all_to_all.10.normed, bf16[256,512]{1,0:T(8,128)(2,1)S(1)} %copy-done.3, f32[16,256]{1,0:T(8,128)S(1)} %copy-done.4, bf16[256,1024]{1,0:T(8,128)(2,1)S(1)} %copy-done.1, ...), custom_call_target="tpu_custom_call" | custom-call | flops 671088640 | bytes 1310720 | tf_op jit(solution)/shard_map/pallas_call | solution.py:290
  28.5 11.9 %all_to_all.11 = bf16[16,32,256]{2,1,0:T(8,128)(2,1)S(1)} all-to-all(bf16[16,32,256]{2,1,0:T(8,128)(2,1)S(1)} %shard_map.152), channel_id=1, replica_groups=mesh['snap'=16,'vert'=32] {'snap'}, dimensions={0} | all-to-all | bytes 524288 | tf_op jit(solution)/shard_map/all_to_all | solution.py:308
  40.5 0.0 copy-start
  40.5 0.0 collective-permute-start.2
  40.5 2.3 %all_gather.7.pair = bf16[1024,256]{1,0:T(8,128)(2,1)S(1)} all-gather(bf16[512,256]{1,0:T(8,128)(2,1)S(1)} %bitcast.10), channel_id=1, replica_groups={{0,1},{2,3},{4,5},{6,7},{8,9},{10,11},{12,13},{14,15},{16,17},{18,19},{..., dimensions={0}, use_global_device_ids=true | all-gather | bytes 786432 | tf_op jit(solution)/shard_map/all_gather | solution.py:206
  42.8 0.0 copy-done
  42.8 0.7 %shard_map.153 = (bf16[512,256]{1,0:T(8,128)(2,1)S(1)}, bf16[512,256]{1,0:T(8,128)(2,1)}, s32[8,128]{1,0:T(8,128)S(1)}) custom-call(s32[1,32]{1,0:T(1,128)} %pair_left.1, s32[1,32]{1,0:T(1,128)} %pair_right.1, bf16[1024,256]{1,0:T(8,128)(2,1)S(1)} %all_gather.7.pair, bf16[256,256]{1,0:T(8,128)(2,1)S(1)} %copy-done), custom_call_target="tpu_custom_call" | custom-call | flops 67108864 | bytes 1048576 | tf_op jit(solution)/shard_map/pallas_call | solution.py:313
  43.5 4.5 %collective-permute-done.2.halo = bf16[512,256]{1,0:T(8,128)(2,1)S(1)} collective-permute-done((bf16[512,256]{1,0:T(8,128)(2,1)S(1)}, bf16[512,256]{1,0:T(8,128)(2,1)S(1)}, u32[]{:S(2)}, u32[]{:S(2)}) %collective-permute-start.2) | collective-permute-done | bytes 262176 | tf_op jit(solution)/shard_map/ppermute | solution.py:200
  48.0 2.0 %shard_map.154 = bf16[32,128,128]{2,1,0:T(8,128)(2,1)} custom-call(s32[8,128]{1,0:T(8,128)S(1)} %get-tuple-element.16.lists, bf16[512,256]{1,0:T(8,128)(2,1)S(1)} %get-tuple-element.17.left, bf16[1024,256]{1,0:T(8,128)(2,1)S(1)} %all_gather.7.pair, bf16[512,256]{1,0:T(8,128)(2,1)S(1)} %collective-permute-done.2.halo), custom_call_target="tpu_custom_call" | custom-call | flops 268435456 | bytes 1048576 | tf_op jit(solution)/shard_map/pallas_call | solution.py:329
Async XLA Ops:
  0.6 8.1 %collective-permute-start = (bf16[512,256]{1,0:T(8,128)(2,1)}, bf16[512,256]{1,0:T(8,128)(2,1)S(1)}, u32[]{:S(2)}, u32[]{:S(2)}) collective-permute-start(bf16[512,256]{1,0:T(8,128)(2,1)} %bitcast.12), channel_id=1, source_target_pairs={{2,0},{4,2},{6,4},{8,6},{10,8},{12,10},{14,12},{16,14},{18,16},{20... | collective-permute-start | bytes 786440 | tf_op jit(solution)/shard_map/ppermute | solution.py:200
  2.9 6.6 %collective-permute-start.1 = (bf16[32,128,128]{2,1,0:T(8,128)(2,1)}, bf16[32,128,128]{2,1,0:T(8,128)(2,1)S(1)}, u32[]{:S(2)}, u32[]{:S(2)}) collective-permute-start(bf16[32,128,128]{2,1,0:T(8,128)(2,1)} %bitcast.14), channel_id=1, source_target_pairs={{0,1},{1,0},{2,3},{3,2},{4,5},{5,4},{6,7},{7,6},{8,9},{9,8},{10,11... | collective-permute-start | bytes 3145736 | tf_op jit(solution)/shard_map/ppermute | solution.py:249
  9.5 17.6 %copy-start.2 = (bf16[1024,256]{1,0:T(8,128)(2,1)S(1)}, bf16[1024,256]{1,0:T(8,128)(2,1)}, u32[]{:S(2)}) copy-start(bf16[1024,256]{1,0:T(8,128)(2,1)} %down.1) | copy-start | bytes 1572868
  9.5 17.6 %copy-start.3 = (bf16[256,512]{1,0:T(8,128)(2,1)S(1)}, bf16[256,512]{1,0:T(8,128)(2,1)}, u32[]{:S(2)}) copy-start(bf16[256,512]{1,0:T(8,128)(2,1)} %mix.1) | copy-start | bytes 786436
  9.5 17.6 %copy-start.4 = (f32[16,256]{1,0:T(8,128)S(1)}, f32[16,256]{1,0:T(8,128)}, u32[]{:S(2)}) copy-start(f32[16,256]{1,0:T(8,128)} %rates.1) | copy-start | bytes 49156
  11.1 16.0 %copy-start.1 = (bf16[256,1024]{1,0:T(8,128)(2,1)S(1)}, bf16[256,1024]{1,0:T(8,128)(2,1)}, u32[]{:S(2)}) copy-start(bf16[256,1024]{1,0:T(8,128)(2,1)} %up.1) | copy-start | bytes 1572868
  40.5 2.3 %copy-start = (bf16[256,256]{1,0:T(8,128)(2,1)S(1)}, bf16[256,256]{1,0:T(8,128)(2,1)}, u32[]{:S(2)}) copy-start(bf16[256,256]{1,0:T(8,128)(2,1)} %link.1) | copy-start | bytes 393220
  40.5 7.6 %collective-permute-start.2 = (bf16[512,256]{1,0:T(8,128)(2,1)S(1)}, bf16[512,256]{1,0:T(8,128)(2,1)S(1)}, u32[]{:S(2)}, u32[]{:S(2)}) collective-permute-start(bf16[512,256]{1,0:T(8,128)(2,1)S(1)} %bitcast.9), channel_id=1, source_target_pairs={{0,2},{2,4},{4,6},{6,8},{8,10},{10,12},{12,14},{14,16},{16,18},{18... | collective-permute-start | bytes 786440 | tf_op jit(solution)/shard_map/ppermute | solution.py:200

commit v5 on v4

--- a/solution.py
+++ b/solution.py
@@ -46,61 +46,72 @@
     return lax.rem(lax.axis_index("vert"), 2)
 
 
-def prepare_kernel(count, src, dst, own, joined, src_near, dst_near, row, sems):
+def prepare_kernel(
+    count,
+    src,
+    dst,
+    own,
+    norm_gain,
+    mlp_gain,
+    joined,
+    norm_gain_out,
+    mlp_gain_out,
+    src_near,
+    dst_near,
+    row,
+    sems,
+):
     vertices, width = own.shape
     slots = src.shape[1]
     lanes = width // 2
-    row[...] = jnp.full(row.shape, count[0, 0], jnp.int32)
     moves = [
         pltpu.make_async_copy(source, target, sems.at[i])
         for i, (source, target) in enumerate(
-            ((src, src_near), (dst, dst_near), (own, joined.at[:vertices]))
+            (
+                (src, src_near),
+                (dst, dst_near),
+                (own, joined.at[:vertices]),
+                (norm_gain, norm_gain_out),
+                (mlp_gain, mlp_gain_out),
+            )
         )
     ]
     for move in moves:
         move.start()
     for move in moves[:2]:
         move.wait()
+    row[...] = jnp.full(row.shape, count[0, 0], jnp.int32)
     row[:, :slots] = src_near[...]
     row[:, lanes : lanes + slots] = dst_near[...]
     trailer = row[...].astype(jnp.float32).astype(joined.dtype)
     joined[vertices:] = jnp.broadcast_to(trailer, (list_rows, width))
-    moves[2].wait()
-
-
-def blocks_kernel(
-    per_part, gain, out_gain, pair, halo, blocks, lists, own, gain_near, out_gain_near, sems
-):
+    for move in moves[2:]:
+        move.wait()
+
+
+def blocks_kernel(per_part, pair, halo, blocks, index, own, lists, sem):
     vertices, width = halo.shape
     stride = pair.shape[0] // 2
     mate = 1 - core_index()
-    loads = [
-        pltpu.make_async_copy(gain, gain_near, sems.at[0]),
-        pltpu.make_async_copy(out_gain, out_gain_near, sems.at[1]),
-    ]
-    for load in loads:
-        load.start()
     place = pl.multiple_of(mate * stride, list_rows)
     start = pl.multiple_of(mate * stride + vertices, list_rows)
     trailer = pair[pl.ds(start, list_rows)].astype(jnp.float32)[:1].astype(jnp.int32)
     lanes = width // 2
     lists[0:1], lists[1:2] = near(trailer[:, lanes:], trailer[:, :lanes], per_part)
     lists[2:3] = trailer[:, :lanes]
+    move = pltpu.make_async_copy(lists, index, sem)
+    move.start()
     blocks[:vertices] = pair[:vertices]
     blocks[vertices : 2 * vertices] = pair[stride : stride + vertices]
     blocks[2 * vertices :] = halo[...]
     own[...] = pair[pl.ds(place, vertices)].astype(jnp.float32)
-    for load in loads:
-        load.wait()
-
-
-def aggregate_kernel(lists, blocks, own, gain, tiles, normed, even, odd, index, sem):
+    move.wait()
+
+
+def aggregate_kernel(index, blocks, own, gain, tiles, normed, even, odd):
     slots, rows, _ = tiles.shape
-    fetch = pltpu.make_async_copy(lists, index, sem)
-    fetch.start()
     even[...] = own[...]
     odd[...] = jnp.zeros_like(odd)
-    fetch.wait()
     live = index[2, slots]
     for k in range(slots):
         total = odd if k % 2 else even
@@ -139,7 +150,18 @@
 
 
 def left_kernel(
-    per_part, pair_left, pair_right, pair, link, left, kept, lists, left_near, right_near, sems
+    per_part,
+    pair_left,
+    pair_right,
+    pair,
+    link,
+    left,
+    kept,
+    index,
+    left_near,
+    right_near,
+    lists,
+    sems,
 ):
     own = block_rows(1 - core_index(), left.shape[0])
     moves = [
@@ -158,17 +180,17 @@
     pairs = left_near.shape[1]
     lists[0:1, :pairs], right = near(left_near[...], right_near[...], per_part)
     lists[1:2, :pairs] = jnp.where(right < 2 * per_part, right ^ per_part, right)
+    fetch = pltpu.make_async_copy(lists, index, sems.at[3])
+    fetch.start()
     moves[2].wait()
-
-
-def score_kernel(lists, left, pair, halo, scores, blocks, tiles, index, fetch_sem, sems):
+    fetch.wait()
+
+
+def score_kernel(index, left, pair, halo, scores, blocks, tiles, sems):
     pairs, rows, _ = scores.shape
     vertices, width = halo.shape
-    fetch = pltpu.make_async_copy(lists, index, fetch_sem)
-    fetch.start()
     blocks[: 2 * vertices] = pair[...]
     blocks[2 * vertices :] = halo[...]
-    fetch.wait()
     batch = pairs // sems.shape[0]
     moves = []
     for k in range(pairs):
@@ -191,6 +213,10 @@
 
 def in_hbm(array):
     return pltpu.with_memory_space_constraint(array, pltpu.HBM)
+
+
+def in_smem(array):
+    return pltpu.with_memory_space_constraint(array, pltpu.SMEM)
 
 
 def zigzag(cells, up):
@@ -233,57 +259,59 @@
     shape = jax.ShapeDtypeStruct
     own = features.reshape(vertices, width)
     halo = zigzag(own, up=False)
-    joined = call(
+    joined, gain, out_gain = call(
         prepare_kernel,
-        shape((vertices + list_rows, width), bf16),
-        VMEM,
-        [SMEM] + [HBM] * 3,
+        (
+            shape((vertices + list_rows, width), bf16),
+            shape((1, width), f32),
+            shape((1, width), f32),
+        ),
+        (VMEM, VMEM, VMEM),
+        [SMEM] + [HBM] * 5,
         (0, 4 * vertices * width, 0),
         [
             pltpu.VMEM((1, slots), jnp.int32),
             pltpu.VMEM((1, slots), jnp.int32),
             pltpu.VMEM((1, width), jnp.int32),
-            pltpu.SemaphoreType.DMA((3,)),
+            pltpu.SemaphoreType.DMA((5,)),
         ],
-    )(tile_count, in_hbm(tile_src), in_hbm(tile_dst), in_hbm(own))
+    )(
+        tile_count,
+        in_hbm(tile_src),
+        in_hbm(tile_dst),
+        in_hbm(own),
+        in_hbm(norm_gain.reshape(1, width)),
+        in_hbm(mlp_gain.reshape(1, width)),
+    )
     tiles = lax.ppermute(
         tile_vals.reshape(slots, rows, rows),
         "vert",
         [(i, i ^ 1) for i in range(lax.axis_size("vert"))],
     )
     pair = chip_pair(joined)
-    blocks, tile_lists, base, gain, out_gain = call(
+    blocks, tile_lists, base = call(
         functools.partial(blocks_kernel, per_part),
         (
             shape((3 * vertices, width), bf16),
-            shape((8, width // 2), jnp.int32),
+            pltpu.SMEM((8, width // 2), jnp.int32),
             shape((vertices, width), f32),
-            shape((1, width), f32),
-            shape((1, width), f32),
-        ),
-        (VMEM,) * 5,
-        [HBM] * 2 + [VMEM] * 2,
+        ),
+        (VMEM, SMEM, VMEM),
+        [VMEM] * 2,
         (2**34, 8 * vertices * width, 0),
-        [pltpu.SemaphoreType.DMA((2,))],
-    )(
-        in_hbm(norm_gain.reshape(1, width)),
-        in_hbm(mlp_gain.reshape(1, width)),
-        pair,
-        halo,
-    )
+        [pltpu.VMEM((8, width // 2), jnp.int32), pltpu.SemaphoreType.DMA],
+    )(pair, halo)
     normed = call(
         aggregate_kernel,
         shape((vertices, width), bf16),
         VMEM,
-        [VMEM] * 5,
+        [SMEM] + [VMEM] * 4,
         (2 * slots * rows * rows * width, 2 * slots * rows * rows, 0),
         [
             pltpu.VMEM((vertices, width), f32),
             pltpu.VMEM((vertices, width), f32),
-            pltpu.SMEM((8, width // 2), jnp.int32),
-            pltpu.SemaphoreType.DMA,
         ],
-    )(tile_lists, blocks, base, gain, tiles)
+    )(in_smem(tile_lists), blocks, base, gain, tiles)
     by_vertex = lax.all_to_all(
         normed.reshape(snaps, vertices // snaps, width), "snap", 0, 0, tiled=True
     )
@@ -315,31 +343,30 @@
         (
             shape((vertices, width), bf16),
             shape((vertices, width), bf16),
-            shape((8, width // 2), jnp.int32),
-        ),
-        (VMEM, ANY, VMEM),
+            pltpu.SMEM((8, width // 2), jnp.int32),
+        ),
+        (VMEM, ANY, SMEM),
         [HBM] * 2 + [VMEM] * 2,
         (2 * vertices * width * width, 8 * vertices * width, 0),
         [
             pltpu.VMEM((1, pairs), jnp.int32),
             pltpu.VMEM((1, pairs), jnp.int32),
-            pltpu.SemaphoreType.DMA((3,)),
+            pltpu.VMEM((8, width // 2), jnp.int32),
+            pltpu.SemaphoreType.DMA((4,)),
         ],
     )(in_hbm(pair_left), in_hbm(pair_right), pair_out, link_weight)
     scores = call(
         score_kernel,
         shape((pairs, rows, rows), bf16),
         ANY,
-        [VMEM] * 4,
+        [SMEM] + [VMEM] * 3,
         (2 * pairs * rows * rows * width, 2 * pairs * rows * rows, 0),
         [
             pltpu.VMEM((3 * vertices, width), bf16),
             pltpu.VMEM((pairs, rows, rows), bf16),
-            pltpu.SMEM((8, width // 2), jnp.int32),
-            pltpu.SemaphoreType.DMA,
             pltpu.SemaphoreType.DMA((8,)),
         ],
-    )(lists, left, pair_out, halo_out)
+    )(in_smem(lists), left, pair_out, halo_out)
     return (
         kept.reshape(1, vertices, width),
         scores.reshape(1, pairs, rows, rows),

time: 50.4 us -> 49.1 us (0.974)
  Pallas kernels: 7.44 us -> 6.81 us
  waiting for transfers between devices: 4.52 us -> 3.92 us
    pallas_call x3, Pallas kernels: 4.61 us -> 3.44 us  [the longest x1 1.49 us: body(): call(score_kernel, shape((pairs, rows, rows), bf16), ANY, [SMEM] + [VMEM]...]
    ppermute x2, waiting for transfers between devices: 4.52 us -> 3.92 us  [zigzag(): lax.ppermute(cells, 'vert', links if up else [(j, i) for i, j in links])]
    pallas_call x1, Pallas kernels: 0.75 us -> 1.35 us  [body(): call(functools.partial(left_kernel, per_part), (shape((vertices, width),...]
  transfers between devices with their start and end apart: 3 -> 3, of which waited for: 1 -> 1; matrix products, arithmetic and copies ran while one was open for 0% -> 0% of each run, Pallas kernels for 5% -> 6%
where the time goes in v5:
time: 49.1 us; the launch traced here: 48.9 us
  blocking collectives  32.6 us (66%)
  Pallas kernels  6.81 us (14%)
  starting transfers between devices  4.14 us (8%)
  waiting for transfers between devices  3.92 us (8%)
  between operations  1.38 us (3%)
    all_to_all x1, blocking collectives, body(): lax.all_to_all(normed.reshape(snaps, vertices // snaps, width), 'snap', 0...  16 us
    all_to_all x1, blocking collectives, body(): lax.all_to_all(vertex_out, 'snap', 0, 0, tiled=True)  11.9 us
    all_gather x2, blocking collectives, chip_pair(): return lax.all_gather(cells, 'vert', axis_index_groups=chips, tiled=True)  4.62 us
    ppermute x2, waiting for transfers between devices, zigzag(): lax.ppermute(cells, 'vert', links if up else [(j, i) for i, j in links])  3.92 us
    ppermute x2, starting transfers between devices, zigzag(): lax.ppermute(cells, 'vert', links if up else [(j, i) for i, j in links])  2.24 us
    ppermute x1, starting transfers between devices, body(): lax.ppermute(tile_vals.reshape(slots, rows, rows), 'vert', [(i, i ^ 1) fo...  1.91 us
    pallas_call x1, Pallas kernels, body(): call(score_kernel, shape((pairs, rows, rows), bf16), ANY, [SMEM] + [VMEM]...  1.49 us
    pallas_call x1, Pallas kernels, body(): call(vertex_kernel, shape(by_vertex.shape, bf16), VMEM, [VMEM] * 6, (2 *...  1.37 us
  transfers between devices with their start and end apart: 3, of which 1 were waited for; matrix products, arithmetic and copies ran while one was open for 0% of the time, Pallas kernels for 6%

profile of v5, /device:TPU:384, one launch (start us, length us, event | category | flops | bytes accessed | tf_op | source)
XLA Modules:
  0.0 48.9 jit_solution(2319597191327515792)
XLA Ops:
  0.6 2.2 %collective-permute-start = (bf16[512,256]{1,0:T(8,128)(2,1)}, bf16[512,256]{1,0:T(8,128)(2,1)S(1)}, u32[]{:S(2)}, u32[]{:S(2)}) collective-permute-start(bf16[512,256]{1,0:T(8,128)(2,1)} %bitcast.12), channel_id=1, source_target_pairs={{2,0},{4,2},{6,4},{8,6},{10,8},{12,10},{14,12},{16,14},{18,16},{20... | collective-permute-start | bytes 786440 | tf_op jit(solution)/shard_map/ppermute | solution.py:226
  2.9 1.9 %collective-permute-start.1 = (bf16[32,128,128]{2,1,0:T(8,128)(2,1)}, bf16[32,128,128]{2,1,0:T(8,128)(2,1)S(1)}, u32[]{:S(2)}, u32[]{:S(2)}) collective-permute-start(bf16[32,128,128]{2,1,0:T(8,128)(2,1)} %bitcast.16), channel_id=1, source_target_pairs={{0,1},{1,0},{2,3},{3,2},{4,5},{5,4},{6,7},{7,6},{8,9},{9,8},{10,11... | collective-permute-start | bytes 3145736 | tf_op jit(solution)/shard_map/ppermute | solution.py:286
  5.4 1.0 %shard_map.149 = (bf16[528,256]{1,0:T(8,128)(2,1)S(1)}, f32[1,256]{1,0:T(1,128)S(1)}, f32[1,256]{1,0:T(1,128)S(1)}) custom-call(s32[1,1]{1,0:T(1,128)S(6)} %copy.16.count, s32[1,32]{1,0:T(1,128)} %src.1, s32[1,32]{1,0:T(1,128)} %dst.1, bf16[512,256]{1,0:T(8,128)(2,1)} %bitcast.13, f32[1,256]{1,0:T(1,128)} %bitcast.14, f32[1,256]{1,0:T(1,128)} %bitcast.15), custom_call_target="tpu_custom_call" | custom-call | bytes 524288 | tf_op jit(solution)/shard_map/pallas_call | solution.py:262
  6.5 2.3 %all_gather.6.pair = bf16[1056,256]{1,0:T(8,128)(2,1)S(1)} all-gather(bf16[528,256]{1,0:T(8,128)(2,1)S(1)} %get-tuple-element.12), channel_id=1, replica_groups={{0,1},{2,3},{4,5},{6,7},{8,9},{10,11},{12,13},{14,15},{16,17},{18,19},{..., dimensions={0}, use_global_device_ids=true | all-gather | bytes 811008 | tf_op jit(solution)/shard_map/all_gather | solution.py:232
  8.8 0.0 collective-permute-done.halo
  8.8 0.6 %shard_map.150 = (bf16[1536,256]{1,0:T(8,128)(2,1)S(1)}, s32[8,128]{1,0:T(8,128)S(4)}, f32[512,256]{1,0:T(8,128)S(1)}) custom-call(bf16[1056,256]{1,0:T(8,128)(2,1)S(1)} %all_gather.6.pair, bf16[512,256]{1,0:T(8,128)(2,1)S(1)} %collective-permute-done.halo), custom_call_target="tpu_custom_call" | custom-call | flops 17179869184 | bytes 1048576 | tf_op jit(solution)/shard_map/pallas_call | solution.py:292
  9.4 0.0 collective-permute-done.1.tiles
  9.4 0.0 copy-start.2
  9.5 0.0 copy-start.3
  9.5 0.0 copy-start.4
  9.5 0.9 %shard_map.151 = bf16[512,256]{1,0:T(8,128)(2,1)S(1)} custom-call(s32[8,128]{1,0:T(8,128)S(4)} %get-tuple-element.13.index, bf16[1536,256]{1,0:T(8,128)(2,1)S(1)} %get-tuple-element.14.blocks, f32[512,256]{1,0:T(8,128)S(1)} %get-tuple-element.15.own, f32[1,256]{1,0:T(1,128)S(1)} %get-tuple-element.16.gain, bf16[32,128,128]{2,1,0:T(8,128)(2,1)S(1)} %collective-permute-done.1.tiles), custom_call_target="tpu_custom_call" | custom-call | flops 268435456 | bytes 1048576 | tf_op jit(solution)/shard_map/pallas_call | solution.py:304
  10.4 0.0 copy-start.1
  10.4 16.0 %all_to_all.10.normed = bf16[16,32,256]{2,1,0:T(8,128)(2,1)S(1)} all-to-all(bf16[16,32,256]{2,1,0:T(8,128)(2,1)S(1)} %bitcast.8), channel_id=1, replica_groups=mesh['snap'=16,'vert'=32] {'snap'}, dimensions={0} | all-to-all | bytes 524288 | tf_op jit(solution)/shard_map/all_to_all | solution.py:315
  26.4 0.0 copy-done.2
  26.4 0.0 copy-done.3
  26.4 0.0 copy-done.4
  26.4 0.0 copy-done.1
  26.5 1.4 %shard_map.152 = bf16[16,32,256]{2,1,0:T(8,128)(2,1)S(1)} custom-call(f32[1,256]{1,0:T(1,128)S(1)} %get-tuple-element.11.gain, bf16[16,32,256]{2,1,0:T(8,128)(2,1)S(1)} %all_to_all.10.normed, bf16[256,512]{1,0:T(8,128)(2,1)S(1)} %copy-done.3, f32[16,256]{1,0:T(8,128)S(1)} %copy-done.4, bf16[256,1024]{1,0:T(8,128)(2,1)S(1)} %copy-done.1, ...), custom_call_target="tpu_custom_call" | custom-call | flops 671088640 | bytes 1310720 | tf_op jit(solution)/shard_map/pallas_call | solution.py:318
  27.8 11.9 %all_to_all.11 = bf16[16,32,256]{2,1,0:T(8,128)(2,1)S(1)} all-to-all(bf16[16,32,256]{2,1,0:T(8,128)(2,1)S(1)} %shard_map.152), channel_id=1, replica_groups=mesh['snap'=16,'vert'=32] {'snap'}, dimensions={0} | all-to-all | bytes 524288 | tf_op jit(solution)/shard_map/all_to_all | solution.py:336
  39.8 0.0 copy-start
  39.8 0.0 collective-permute-start.2
  39.8 2.3 %all_gather.7.pair = bf16[1024,256]{1,0:T(8,128)(2,1)S(1)} all-gather(bf16[512,256]{1,0:T(8,128)(2,1)S(1)} %bitcast.10), channel_id=1, replica_groups={{0,1},{2,3},{4,5},{6,7},{8,9},{10,11},{12,13},{14,15},{16,17},{18,19},{..., dimensions={0}, use_global_device_ids=true | all-gather | bytes 786432 | tf_op jit(solution)/shard_map/all_gather | solution.py:232
  42.1 0.0 copy-done
  42.1 1.4 %shard_map.153 = (bf16[512,256]{1,0:T(8,128)(2,1)S(1)}, bf16[512,256]{1,0:T(8,128)(2,1)}, s32[8,128]{1,0:T(8,128)S(4)}) custom-call(s32[1,32]{1,0:T(1,128)} %pair_left.1, s32[1,32]{1,0:T(1,128)} %pair_right.1, bf16[1024,256]{1,0:T(8,128)(2,1)S(1)} %all_gather.7.pair, bf16[256,256]{1,0:T(8,128)(2,1)S(1)} %copy-done), custom_call_target="tpu_custom_call" | custom-call | flops 67108864 | bytes 1048576 | tf_op jit(solution)/shard_map/pallas_call | solution.py:341
  43.4 3.9 %collective-permute-done.2.halo = bf16[512,256]{1,0:T(8,128)(2,1)S(1)} collective-permute-done((bf16[512,256]{1,0:T(8,128)(2,1)S(1)}, bf16[512,256]{1,0:T(8,128)(2,1)S(1)}, u32[]{:S(2)}, u32[]{:S(2)}) %collective-permute-start.2) | collective-permute-done | bytes 262176 | tf_op jit(solution)/shard_map/ppermute | solution.py:226
  47.4 1.5 %shard_map.154 = bf16[32,128,128]{2,1,0:T(8,128)(2,1)} custom-call(s32[8,128]{1,0:T(8,128)S(4)} %get-tuple-element.18.index, bf16[512,256]{1,0:T(8,128)(2,1)S(1)} %get-tuple-element.19.left, bf16[1024,256]{1,0:T(8,128)(2,1)S(1)} %all_gather.7.pair, bf16[512,256]{1,0:T(8,128)(2,1)S(1)} %collective-permute-done.2.halo), custom_call_target="tpu_custom_call" | custom-call | flops 268435456 | bytes 1048576 | tf_op jit(solution)/shard_map/pallas_call | solution.py:358
Async XLA Ops:
  0.6 8.2 %collective-permute-start = (bf16[512,256]{1,0:T(8,128)(2,1)}, bf16[512,256]{1,0:T(8,128)(2,1)S(1)}, u32[]{:S(2)}, u32[]{:S(2)}) collective-permute-start(bf16[512,256]{1,0:T(8,128)(2,1)} %bitcast.12), channel_id=1, source_target_pairs={{2,0},{4,2},{6,4},{8,6},{10,8},{12,10},{14,12},{16,14},{18,16},{20... | collective-permute-start | bytes 786440 | tf_op jit(solution)/shard_map/ppermute | solution.py:226
  2.9 6.6 %collective-permute-start.1 = (bf16[32,128,128]{2,1,0:T(8,128)(2,1)}, bf16[32,128,128]{2,1,0:T(8,128)(2,1)S(1)}, u32[]{:S(2)}, u32[]{:S(2)}) collective-permute-start(bf16[32,128,128]{2,1,0:T(8,128)(2,1)} %bitcast.16), channel_id=1, source_target_pairs={{0,1},{1,0},{2,3},{3,2},{4,5},{5,4},{6,7},{7,6},{8,9},{9,8},{10,11... | collective-permute-start | bytes 3145736 | tf_op jit(solution)/shard_map/ppermute | solution.py:286
  9.4 17.0 %copy-start.2 = (bf16[1024,256]{1,0:T(8,128)(2,1)S(1)}, bf16[1024,256]{1,0:T(8,128)(2,1)}, u32[]{:S(2)}) copy-start(bf16[1024,256]{1,0:T(8,128)(2,1)} %down.1) | copy-start | bytes 1572868
  9.5 17.0 %copy-start.3 = (bf16[256,512]{1,0:T(8,128)(2,1)S(1)}, bf16[256,512]{1,0:T(8,128)(2,1)}, u32[]{:S(2)}) copy-start(bf16[256,512]{1,0:T(8,128)(2,1)} %mix.1) | copy-start | bytes 786436
  9.5 17.0 %copy-start.4 = (f32[16,256]{1,0:T(8,128)S(1)}, f32[16,256]{1,0:T(8,128)}, u32[]{:S(2)}) copy-start(f32[16,256]{1,0:T(8,128)} %rates.1) | copy-start | bytes 49156
  10.4 16.0 %copy-start.1 = (bf16[256,1024]{1,0:T(8,128)(2,1)S(1)}, bf16[256,1024]{1,0:T(8,128)(2,1)}, u32[]{:S(2)}) copy-start(bf16[256,1024]{1,0:T(8,128)(2,1)} %up.1) | copy-start | bytes 1572868
  39.8 2.3 %copy-start = (bf16[256,256]{1,0:T(8,128)(2,1)S(1)}, bf16[256,256]{1,0:T(8,128)(2,1)}, u32[]{:S(2)}) copy-start(bf16[256,256]{1,0:T(8,128)(2,1)} %link.1) | copy-start | bytes 393220
  39.8 7.6 %collective-permute-start.2 = (bf16[512,256]{1,0:T(8,128)(2,1)S(1)}, bf16[512,256]{1,0:T(8,128)(2,1)S(1)}, u32[]{:S(2)}, u32[]{:S(2)}) collective-permute-start(bf16[512,256]{1,0:T(8,128)(2,1)S(1)} %bitcast.9), channel_id=1, source_target_pairs={{0,2},{2,4},{4,6},{6,8},{8,10},{10,12},{12,14},{14,16},{16,18},{18... | collective-permute-start | bytes 786440 | tf_op jit(solution)/shard_map/ppermute | solution.py:226

commit v6 on v5

--- a/solution.py
+++ b/solution.py
@@ -17,7 +17,7 @@
 HBM = pl.BlockSpec(memory_space=pltpu.HBM)
 
 
-def call(kernel, outs, out_specs, in_specs, cost, scratch=()):
+def call(kernel, outs, out_specs, in_specs, cost, scratch=(), aliases=None):
     flops, bytes_accessed, transcendentals = cost
     return pl.pallas_call(
         kernel,
@@ -25,6 +25,7 @@
         in_specs=in_specs,
         out_specs=out_specs,
         scratch_shapes=list(scratch),
+        input_output_aliases=aliases or {},
         compiler_params=pltpu.CompilerParams(vmem_limit_bytes=40 * 2**20),
         cost_estimate=pl.CostEstimate(
             flops=flops, bytes_accessed=bytes_accessed, transcendentals=transcendentals
@@ -89,11 +90,10 @@
         move.wait()
 
 
-def blocks_kernel(per_part, pair, halo, blocks, index, own, lists, sem):
+def blocks_kernel(per_part, pair, halo, blocks, index, lists, sem):
     vertices, width = halo.shape
     stride = pair.shape[0] // 2
     mate = 1 - core_index()
-    place = pl.multiple_of(mate * stride, list_rows)
     start = pl.multiple_of(mate * stride + vertices, list_rows)
     trailer = pair[pl.ds(start, list_rows)].astype(jnp.float32)[:1].astype(jnp.int32)
     lanes = width // 2
@@ -104,13 +104,13 @@
     blocks[:vertices] = pair[:vertices]
     blocks[vertices : 2 * vertices] = pair[stride : stride + vertices]
     blocks[2 * vertices :] = halo[...]
-    own[...] = pair[pl.ds(place, vertices)].astype(jnp.float32)
     move.wait()
 
 
-def aggregate_kernel(index, blocks, own, gain, tiles, normed, even, odd):
+def aggregate_kernel(index, blocks, gain, tiles, normed, even, odd):
     slots, rows, _ = tiles.shape
-    even[...] = own[...]
+    own = block_rows(1 - core_index(), even.shape[0])
+    even[...] = blocks[own].astype(jnp.float32)
     odd[...] = jnp.zeros_like(odd)
     live = index[2, slots]
     for k in range(slots):
@@ -158,6 +158,7 @@
     left,
     kept,
     index,
+    blocks,
     left_near,
     right_near,
     lists,
@@ -182,14 +183,15 @@
     lists[1:2, :pairs] = jnp.where(right < 2 * per_part, right ^ per_part, right)
     fetch = pltpu.make_async_copy(lists, index, sems.at[3])
     fetch.start()
+    blocks[: pair.shape[0]] = pair[...]
     moves[2].wait()
     fetch.wait()
 
 
-def score_kernel(index, left, pair, halo, scores, blocks, tiles, sems):
+def score_kernel(index, left, halo, table, scores, blocks, tiles, sems):
     pairs, rows, _ = scores.shape
     vertices, width = halo.shape
-    blocks[: 2 * vertices] = pair[...]
+    del table
     blocks[2 * vertices :] = halo[...]
     batch = pairs // sems.shape[0]
     moves = []
@@ -289,14 +291,13 @@
         [(i, i ^ 1) for i in range(lax.axis_size("vert"))],
     )
     pair = chip_pair(joined)
-    blocks, tile_lists, base = call(
+    blocks, tile_lists = call(
         functools.partial(blocks_kernel, per_part),
         (
             shape((3 * vertices, width), bf16),
             pltpu.SMEM((8, width // 2), jnp.int32),
-            shape((vertices, width), f32),
-        ),
-        (VMEM, SMEM, VMEM),
+        ),
+        (VMEM, SMEM),
         [VMEM] * 2,
         (2**34, 8 * vertices * width, 0),
         [pltpu.VMEM((8, width // 2), jnp.int32), pltpu.SemaphoreType.DMA],
@@ -305,13 +306,13 @@
         aggregate_kernel,
         shape((vertices, width), bf16),
         VMEM,
-        [SMEM] + [VMEM] * 4,
+        [SMEM] + [VMEM] * 3,
         (2 * slots * rows * rows * width, 2 * slots * rows * rows, 0),
         [
             pltpu.VMEM((vertices, width), f32),
             pltpu.VMEM((vertices, width), f32),
         ],
-    )(in_smem(tile_lists), blocks, base, gain, tiles)
+    )(in_smem(tile_lists), blocks, gain, tiles)
     by_vertex = lax.all_to_all(
         normed.reshape(snaps, vertices // snaps, width), "snap", 0, 0, tiled=True
     )
@@ -338,14 +339,15 @@
     )
     halo_out = zigzag(embeddings, up=True)
     pair_out = chip_pair(embeddings)
-    left, kept, lists = call(
+    left, kept, lists, table = call(
         functools.partial(left_kernel, per_part),
         (
             shape((vertices, width), bf16),
             shape((vertices, width), bf16),
             pltpu.SMEM((8, width // 2), jnp.int32),
-        ),
-        (VMEM, ANY, SMEM),
+            shape((3 * vertices, width), bf16),
+        ),
+        (VMEM, ANY, SMEM, VMEM),
         [HBM] * 2 + [VMEM] * 2,
         (2 * vertices * width * width, 8 * vertices * width, 0),
         [
@@ -355,18 +357,15 @@
             pltpu.SemaphoreType.DMA((4,)),
         ],
     )(in_hbm(pair_left), in_hbm(pair_right), pair_out, link_weight)
-    scores = call(
+    scores, _ = call(
         score_kernel,
-        shape((pairs, rows, rows), bf16),
-        ANY,
+        (shape((pairs, rows, rows), bf16), shape(table.shape, bf16)),
+        (ANY, VMEM),
         [SMEM] + [VMEM] * 3,
         (2 * pairs * rows * rows * width, 2 * pairs * rows * rows, 0),
-        [
-            pltpu.VMEM((3 * vertices, width), bf16),
-            pltpu.VMEM((pairs, rows, rows), bf16),
-            pltpu.SemaphoreType.DMA((8,)),
-        ],
-    )(in_smem(lists), left, pair_out, halo_out)
+        [pltpu.VMEM((pairs, rows, rows), bf16), pltpu.SemaphoreType.DMA((8,))],
+        {3: 1},
+    )(in_smem(lists), left, halo_out, table)
     return (
         kept.reshape(1, vertices, width),
         scores.reshape(1, pairs, rows, rows),

time: 49.1 us -> 49.1 us (level)
  no operation moved by 1% of the time
where the time goes in v6:
time: 49.1 us; the launch traced here: 48.8 us
  blocking collectives  32.6 us (66%)
  Pallas kernels  6.75 us (14%)
  starting transfers between devices  4.14 us (8%)
  waiting for transfers between devices  3.92 us (8%)
  between operations  1.38 us (3%)
    all_to_all x1, blocking collectives, body(): lax.all_to_all(normed.reshape(snaps, vertices // snaps, width), 'snap', 0...  16 us
    all_to_all x1, blocking collectives, body(): lax.all_to_all(vertex_out, 'snap', 0, 0, tiled=True)  11.9 us
    all_gather x2, blocking collectives, chip_pair(): return lax.all_gather(cells, 'vert', axis_index_groups=chips, tiled=True)  4.62 us
    ppermute x2, waiting for transfers between devices, zigzag(): lax.ppermute(cells, 'vert', links if up else [(j, i) for i, j in links])  3.91 us
    ppermute x2, starting transfers between devices, zigzag(): lax.ppermute(cells, 'vert', links if up else [(j, i) for i, j in links])  2.24 us
    ppermute x1, starting transfers between devices, body(): lax.ppermute(tile_vals.reshape(slots, rows, rows), 'vert', [(i, i ^ 1) fo...  1.91 us
    pallas_call x1, Pallas kernels, body(): call(score_kernel, (shape((pairs, rows, rows), bf16), shape(table.shape,...  1.46 us
    pallas_call x1, Pallas kernels, body(): call(vertex_kernel, shape(by_vertex.shape, bf16), VMEM, [VMEM] * 6, (2 *...  1.37 us
  transfers between devices with their start and end apart: 3, of which 1 were waited for; matrix products, arithmetic and copies ran while one was open for 0% of the time, Pallas kernels for 6%

profile of v6, /device:TPU:384, one launch (start us, length us, event | category | flops | bytes accessed | tf_op | source)
XLA Modules:
  0.0 48.8 jit_solution(8803378438461957166)
XLA Ops:
  0.6 2.2 %collective-permute-start = (bf16[512,256]{1,0:T(8,128)(2,1)}, bf16[512,256]{1,0:T(8,128)(2,1)S(1)}, u32[]{:S(2)}, u32[]{:S(2)}) collective-permute-start(bf16[512,256]{1,0:T(8,128)(2,1)} %bitcast.11), channel_id=1, source_target_pairs={{2,0},{4,2},{6,4},{8,6},{10,8},{12,10},{14,12},{16,14},{18,16},{20... | collective-permute-start | bytes 786440 | tf_op jit(solution)/shard_map/ppermute | solution.py:228
  2.9 1.9 %collective-permute-start.1 = (bf16[32,128,128]{2,1,0:T(8,128)(2,1)}, bf16[32,128,128]{2,1,0:T(8,128)(2,1)S(1)}, u32[]{:S(2)}, u32[]{:S(2)}) collective-permute-start(bf16[32,128,128]{2,1,0:T(8,128)(2,1)} %bitcast.15), channel_id=1, source_target_pairs={{0,1},{1,0},{2,3},{3,2},{4,5},{5,4},{6,7},{7,6},{8,9},{9,8},{10,11... | collective-permute-start | bytes 3145736 | tf_op jit(solution)/shard_map/ppermute | solution.py:288
  5.4 1.0 %shard_map.149 = (bf16[528,256]{1,0:T(8,128)(2,1)S(1)}, f32[1,256]{1,0:T(1,128)S(1)}, f32[1,256]{1,0:T(1,128)S(1)}) custom-call(s32[1,1]{1,0:T(1,128)S(6)} %copy.18.count, s32[1,32]{1,0:T(1,128)} %src.1, s32[1,32]{1,0:T(1,128)} %dst.1, bf16[512,256]{1,0:T(8,128)(2,1)} %bitcast.12, f32[1,256]{1,0:T(1,128)} %bitcast.13, f32[1,256]{1,0:T(1,128)} %bitcast.14), custom_call_target="tpu_custom_call" | custom-call | bytes 524288 | tf_op jit(solution)/shard_map/pallas_call | solution.py:264
  6.5 2.3 %all_gather.6.pair = bf16[1056,256]{1,0:T(8,128)(2,1)S(1)} all-gather(bf16[528,256]{1,0:T(8,128)(2,1)S(1)} %get-tuple-element.13), channel_id=1, replica_groups={{0,1},{2,3},{4,5},{6,7},{8,9},{10,11},{12,13},{14,15},{16,17},{18,19},{..., dimensions={0}, use_global_device_ids=true | all-gather | bytes 811008 | tf_op jit(solution)/shard_map/all_gather | solution.py:234
  8.8 0.0 collective-permute-done.halo
  8.8 0.6 %shard_map.150 = (bf16[1536,256]{1,0:T(8,128)(2,1)S(1)}, s32[8,128]{1,0:T(8,128)S(4)}) custom-call(bf16[1056,256]{1,0:T(8,128)(2,1)S(1)} %all_gather.6.pair, bf16[512,256]{1,0:T(8,128)(2,1)S(1)} %collective-permute-done.halo), custom_call_target="tpu_custom_call" | custom-call | flops 17179869184 | bytes 1048576 | tf_op jit(solution)/shard_map/pallas_call | solution.py:294
  9.4 0.0 collective-permute-done.1.tiles
  9.4 0.0 copy-start.2
  9.5 0.0 copy-start.3
  9.5 0.0 copy-start.4
  9.5 0.9 %shard_map.151 = bf16[512,256]{1,0:T(8,128)(2,1)S(1)} custom-call(s32[8,128]{1,0:T(8,128)S(4)} %get-tuple-element.14.index, bf16[1536,256]{1,0:T(8,128)(2,1)S(1)} %get-tuple-element.15.blocks, f32[1,256]{1,0:T(1,128)S(1)} %get-tuple-element.16.gain, bf16[32,128,128]{2,1,0:T(8,128)(2,1)S(1)} %collective-permute-done.1.tiles), custom_call_target="tpu_custom_call" | custom-call | flops 268435456 | bytes 1048576 | tf_op jit(solution)/shard_map/pallas_call | solution.py:305
  10.4 0.0 copy-start.1
  10.4 16.0 %all_to_all.10.normed = bf16[16,32,256]{2,1,0:T(8,128)(2,1)S(1)} all-to-all(bf16[16,32,256]{2,1,0:T(8,128)(2,1)S(1)} %bitcast.8), channel_id=1, replica_groups=mesh['snap'=16,'vert'=32] {'snap'}, dimensions={0} | all-to-all | bytes 524288 | tf_op jit(solution)/shard_map/all_to_all | solution.py:316
  26.4 0.0 copy-done.2
  26.4 0.0 copy-done.3
  26.4 0.0 copy-done.4
  26.4 0.0 copy-done.1
  26.4 1.4 %shard_map.152 = bf16[16,32,256]{2,1,0:T(8,128)(2,1)S(1)} custom-call(f32[1,256]{1,0:T(1,128)S(1)} %get-tuple-element.12.gain, bf16[16,32,256]{2,1,0:T(8,128)(2,1)S(1)} %all_to_all.10.normed, bf16[256,512]{1,0:T(8,128)(2,1)S(1)} %copy-done.3, f32[16,256]{1,0:T(8,128)S(1)} %copy-done.4, bf16[256,1024]{1,0:T(8,128)(2,1)S(1)} %copy-done.1, ...), custom_call_target="tpu_custom_call" | custom-call | flops 671088640 | bytes 1310720 | tf_op jit(solution)/shard_map/pallas_call | solution.py:319
  27.8 11.9 %all_to_all.11 = bf16[16,32,256]{2,1,0:T(8,128)(2,1)S(1)} all-to-all(bf16[16,32,256]{2,1,0:T(8,128)(2,1)S(1)} %shard_map.152), channel_id=1, replica_groups=mesh['snap'=16,'vert'=32] {'snap'}, dimensions={0} | all-to-all | bytes 524288 | tf_op jit(solution)/shard_map/all_to_all | solution.py:337
  39.8 0.0 copy-start
  39.8 0.0 collective-permute-start.2
  39.8 2.3 %all_gather.7.pair = bf16[1024,256]{1,0:T(8,128)(2,1)S(1)} all-gather(bf16[512,256]{1,0:T(8,128)(2,1)S(1)} %bitcast.10), channel_id=1, replica_groups={{0,1},{2,3},{4,5},{6,7},{8,9},{10,11},{12,13},{14,15},{16,17},{18,19},{..., dimensions={0}, use_global_device_ids=true | all-gather | bytes 786432 | tf_op jit(solution)/shard_map/all_gather | solution.py:234
  42.1 0.0 copy-done
  42.1 1.4 %shard_map.153 = (bf16[512,256]{1,0:T(8,128)(2,1)S(1)}, bf16[512,256]{1,0:T(8,128)(2,1)}, s32[8,128]{1,0:T(8,128)S(4)}, bf16[1536,256]{1,0:T(8,128)(2,1)S(1)}) custom-call(s32[1,32]{1,0:T(1,128)} %pair_left.1, s32[1,32]{1,0:T(1,128)} %pair_right.1, bf16[1024,256]{1,0:T(8,128)(2,1)S(1)} %all_gather.7.pair, bf16[256,256]{1,0:T(8,128)(2,1)S(1)} %copy-done), custom_call_target="tpu_custom_call" | custom-call | flops 67108864 | bytes 1048576 | tf_op jit(solution)/shard_map/pallas_call | solution.py:342
  43.4 3.9 %collective-permute-done.2.halo = bf16[512,256]{1,0:T(8,128)(2,1)S(1)} collective-permute-done((bf16[512,256]{1,0:T(8,128)(2,1)S(1)}, bf16[512,256]{1,0:T(8,128)(2,1)S(1)}, u32[]{:S(2)}, u32[]{:S(2)}) %collective-permute-start.2) | collective-permute-done | bytes 262176 | tf_op jit(solution)/shard_map/ppermute | solution.py:228
  47.3 1.5 %shard_map.154 = (bf16[32,128,128]{2,1,0:T(8,128)(2,1)}, bf16[1536,256]{1,0:T(8,128)(2,1)S(1)}) custom-call(s32[8,128]{1,0:T(8,128)S(4)} %get-tuple-element.18.index, bf16[512,256]{1,0:T(8,128)(2,1)S(1)} %get-tuple-element.19.left, bf16[512,256]{1,0:T(8,128)(2,1)S(1)} %collective-permute-done.2.halo, ...), custom_call_target="tpu_custom_call", output_to_operand_aliasing={{1}: (3, {})} | custom-call | flops 268435456 | bytes 1048576 | tf_op jit(solution)/shard_map/pallas_call | solution.py:360
Async XLA Ops:
  0.6 8.2 %collective-permute-start = (bf16[512,256]{1,0:T(8,128)(2,1)}, bf16[512,256]{1,0:T(8,128)(2,1)S(1)}, u32[]{:S(2)}, u32[]{:S(2)}) collective-permute-start(bf16[512,256]{1,0:T(8,128)(2,1)} %bitcast.11), channel_id=1, source_target_pairs={{2,0},{4,2},{6,4},{8,6},{10,8},{12,10},{14,12},{16,14},{18,16},{20... | collective-permute-start | bytes 786440 | tf_op jit(solution)/shard_map/ppermute | solution.py:228
  2.9 6.6 %collective-permute-start.1 = (bf16[32,128,128]{2,1,0:T(8,128)(2,1)}, bf16[32,128,128]{2,1,0:T(8,128)(2,1)S(1)}, u32[]{:S(2)}, u32[]{:S(2)}) collective-permute-start(bf16[32,128,128]{2,1,0:T(8,128)(2,1)} %bitcast.15), channel_id=1, source_target_pairs={{0,1},{1,0},{2,3},{3,2},{4,5},{5,4},{6,7},{7,6},{8,9},{9,8},{10,11... | collective-permute-start | bytes 3145736 | tf_op jit(solution)/shard_map/ppermute | solution.py:288
  9.4 17.0 %copy-start.2 = (bf16[1024,256]{1,0:T(8,128)(2,1)S(1)}, bf16[1024,256]{1,0:T(8,128)(2,1)}, u32[]{:S(2)}) copy-start(bf16[1024,256]{1,0:T(8,128)(2,1)} %down.1) | copy-start | bytes 1572868
  9.5 17.0 %copy-start.3 = (bf16[256,512]{1,0:T(8,128)(2,1)S(1)}, bf16[256,512]{1,0:T(8,128)(2,1)}, u32[]{:S(2)}) copy-start(bf16[256,512]{1,0:T(8,128)(2,1)} %mix.1) | copy-start | bytes 786436
  9.5 16.9 %copy-start.4 = (f32[16,256]{1,0:T(8,128)S(1)}, f32[16,256]{1,0:T(8,128)}, u32[]{:S(2)}) copy-start(f32[16,256]{1,0:T(8,128)} %rates.1) | copy-start | bytes 49156
  10.4 16.0 %copy-start.1 = (bf16[256,1024]{1,0:T(8,128)(2,1)S(1)}, bf16[256,1024]{1,0:T(8,128)(2,1)}, u32[]{:S(2)}) copy-start(bf16[256,1024]{1,0:T(8,128)(2,1)} %up.1) | copy-start | bytes 1572868
  39.8 2.3 %copy-start = (bf16[256,256]{1,0:T(8,128)(2,1)S(1)}, bf16[256,256]{1,0:T(8,128)(2,1)}, u32[]{:S(2)}) copy-start(bf16[256,256]{1,0:T(8,128)(2,1)} %link.1) | copy-start | bytes 393220
  39.8 7.6 %collective-permute-start.2 = (bf16[512,256]{1,0:T(8,128)(2,1)S(1)}, bf16[512,256]{1,0:T(8,128)(2,1)S(1)}, u32[]{:S(2)}, u32[]{:S(2)}) collective-permute-start(bf16[512,256]{1,0:T(8,128)(2,1)S(1)} %bitcast.9), channel_id=1, source_target_pairs={{0,2},{2,4},{4,6},{6,8},{8,10},{10,12},{12,14},{14,16},{16,18},{18... | collective-permute-start | bytes 786440 | tf_op jit(solution)/shard_map/ppermute | solution.py:228

commit v7 on v5

--- a/solution.py
+++ b/solution.py
@@ -89,11 +89,10 @@
         move.wait()
 
 
-def blocks_kernel(per_part, pair, halo, blocks, index, own, lists, sem):
+def blocks_kernel(per_part, pair, halo, blocks, index, lists, sem):
     vertices, width = halo.shape
     stride = pair.shape[0] // 2
     mate = 1 - core_index()
-    place = pl.multiple_of(mate * stride, list_rows)
     start = pl.multiple_of(mate * stride + vertices, list_rows)
     trailer = pair[pl.ds(start, list_rows)].astype(jnp.float32)[:1].astype(jnp.int32)
     lanes = width // 2
@@ -104,13 +103,13 @@
     blocks[:vertices] = pair[:vertices]
     blocks[vertices : 2 * vertices] = pair[stride : stride + vertices]
     blocks[2 * vertices :] = halo[...]
-    own[...] = pair[pl.ds(place, vertices)].astype(jnp.float32)
     move.wait()
 
 
-def aggregate_kernel(index, blocks, own, gain, tiles, normed, even, odd):
+def aggregate_kernel(index, blocks, gain, tiles, normed, even, odd):
     slots, rows, _ = tiles.shape
-    even[...] = own[...]
+    own = block_rows(1 - core_index(), even.shape[0])
+    even[...] = blocks[own].astype(jnp.float32)
     odd[...] = jnp.zeros_like(odd)
     live = index[2, slots]
     for k in range(slots):
@@ -132,7 +131,7 @@
         mix[...],
         preferred_element_type=jnp.float32,
     )
-    gate = 1.0 / (1.0 + jnp.exp(-projected[:, :width]))
+    gate = 0.5 + 0.5 * jnp.tanh(0.5 * projected[:, :width])
     state = jnp.zeros((rows, width), jnp.float32)
     states = []
     for step in range(steps):
@@ -144,7 +143,8 @@
     scale = lax.rsqrt(jnp.mean(states * states, axis=-1, keepdims=True) + epsilon)
     state_normed = (states * scale * gain[...]).astype(jnp.bfloat16)
     inner = jnp.dot(state_normed, up[...], preferred_element_type=jnp.float32)
-    hidden = (inner / (1.0 + jnp.exp(-inner))).astype(jnp.bfloat16)
+    half = 0.5 * inner
+    hidden = (half + half * jnp.tanh(half)).astype(jnp.bfloat16)
     result = states + jnp.dot(hidden, down[...], preferred_element_type=jnp.float32)
     out[...] = result.astype(out.dtype).reshape(steps, rows, width)
 
@@ -289,14 +289,13 @@
         [(i, i ^ 1) for i in range(lax.axis_size("vert"))],
     )
     pair = chip_pair(joined)
-    blocks, tile_lists, base = call(
+    blocks, tile_lists = call(
         functools.partial(blocks_kernel, per_part),
         (
             shape((3 * vertices, width), bf16),
             pltpu.SMEM((8, width // 2), jnp.int32),
-            shape((vertices, width), f32),
-        ),
-        (VMEM, SMEM, VMEM),
+        ),
+        (VMEM, SMEM),
         [VMEM] * 2,
         (2**34, 8 * vertices * width, 0),
         [pltpu.VMEM((8, width // 2), jnp.int32), pltpu.SemaphoreType.DMA],
@@ -305,13 +304,13 @@
         aggregate_kernel,
         shape((vertices, width), bf16),
         VMEM,
-        [SMEM] + [VMEM] * 4,
+        [SMEM] + [VMEM] * 3,
         (2 * slots * rows * rows * width, 2 * slots * rows * rows, 0),
         [
             pltpu.VMEM((vertices, width), f32),
             pltpu.VMEM((vertices, width), f32),
         ],
-    )(in_smem(tile_lists), blocks, base, gain, tiles)
+    )(in_smem(tile_lists), blocks, gain, tiles)
     by_vertex = lax.all_to_all(
         normed.reshape(snaps, vertices // snaps, width), "snap", 0, 0, tiled=True
     )

time: 49.1 us -> 49 us (level)
  no operation moved by 1% of the time
where the time goes in v7:
time: 49 us; the launch traced here: 48.8 us
  blocking collectives  32.6 us (67%)
  Pallas kernels  6.72 us (14%)
  starting transfers between devices  4.14 us (8%)
  waiting for transfers between devices  3.92 us (8%)
  between operations  1.38 us (3%)
    all_to_all x1, blocking collectives, body(): lax.all_to_all(normed.reshape(snaps, vertices // snaps, width), 'snap', 0...  16 us
    all_to_all x1, blocking collectives, body(): lax.all_to_all(vertex_out, 'snap', 0, 0, tiled=True)  11.9 us
    all_gather x2, blocking collectives, chip_pair(): return lax.all_gather(cells, 'vert', axis_index_groups=chips, tiled=True)  4.62 us
    ppermute x2, waiting for transfers between devices, zigzag(): lax.ppermute(cells, 'vert', links if up else [(j, i) for i, j in links])  3.92 us
    ppermute x2, starting transfers between devices, zigzag(): lax.ppermute(cells, 'vert', links if up else [(j, i) for i, j in links])  2.24 us
    ppermute x1, starting transfers between devices, body(): lax.ppermute(tile_vals.reshape(slots, rows, rows), 'vert', [(i, i ^ 1) fo...  1.91 us
    pallas_call x1, Pallas kernels, body(): call(score_kernel, shape((pairs, rows, rows), bf16), ANY, [SMEM] + [VMEM]...  1.49 us
    pallas_call x1, Pallas kernels, body(): call(functools.partial(left_kernel, per_part), (shape((vertices, width),...  1.35 us
  transfers between devices with their start and end apart: 3, of which 1 were waited for; matrix products, arithmetic and copies ran while one was open for 0% of the time, Pallas kernels for 6%

profile of v7, /device:TPU:384, one launch (start us, length us, event | category | flops | bytes accessed | tf_op | source)
XLA Modules:
  0.0 48.8 jit_solution(15894137890316404006)
XLA Ops:
  0.6 2.2 %collective-permute-start = (bf16[512,256]{1,0:T(8,128)(2,1)}, bf16[512,256]{1,0:T(8,128)(2,1)S(1)}, u32[]{:S(2)}, u32[]{:S(2)}) collective-permute-start(bf16[512,256]{1,0:T(8,128)(2,1)} %bitcast.12), channel_id=1, source_target_pairs={{2,0},{4,2},{6,4},{8,6},{10,8},{12,10},{14,12},{16,14},{18,16},{20... | collective-permute-start | bytes 786440 | tf_op jit(solution)/shard_map/ppermute | solution.py:226
  2.9 1.9 %collective-permute-start.1 = (bf16[32,128,128]{2,1,0:T(8,128)(2,1)}, bf16[32,128,128]{2,1,0:T(8,128)(2,1)S(1)}, u32[]{:S(2)}, u32[]{:S(2)}) collective-permute-start(bf16[32,128,128]{2,1,0:T(8,128)(2,1)} %bitcast.16), channel_id=1, source_target_pairs={{0,1},{1,0},{2,3},{3,2},{4,5},{5,4},{6,7},{7,6},{8,9},{9,8},{10,11... | collective-permute-start | bytes 3145736 | tf_op jit(solution)/shard_map/ppermute | solution.py:286
  5.4 1.0 %shard_map.149 = (bf16[528,256]{1,0:T(8,128)(2,1)S(1)}, f32[1,256]{1,0:T(1,128)S(1)}, f32[1,256]{1,0:T(1,128)S(1)}) custom-call(s32[1,1]{1,0:T(1,128)S(6)} %copy.16.count, s32[1,32]{1,0:T(1,128)} %src.1, s32[1,32]{1,0:T(1,128)} %dst.1, bf16[512,256]{1,0:T(8,128)(2,1)} %bitcast.13, f32[1,256]{1,0:T(1,128)} %bitcast.14, f32[1,256]{1,0:T(1,128)} %bitcast.15), custom_call_target="tpu_custom_call" | custom-call | bytes 524288 | tf_op jit(solution)/shard_map/pallas_call | solution.py:262
  6.5 2.3 %all_gather.6.pair = bf16[1056,256]{1,0:T(8,128)(2,1)S(1)} all-gather(bf16[528,256]{1,0:T(8,128)(2,1)S(1)} %get-tuple-element.11), channel_id=1, replica_groups={{0,1},{2,3},{4,5},{6,7},{8,9},{10,11},{12,13},{14,15},{16,17},{18,19},{..., dimensions={0}, use_global_device_ids=true | all-gather | bytes 811008 | tf_op jit(solution)/shard_map/all_gather | solution.py:232
  8.8 0.0 collective-permute-done.halo
  8.8 0.6 %shard_map.150 = (bf16[1536,256]{1,0:T(8,128)(2,1)S(1)}, s32[8,128]{1,0:T(8,128)S(4)}) custom-call(bf16[1056,256]{1,0:T(8,128)(2,1)S(1)} %all_gather.6.pair, bf16[512,256]{1,0:T(8,128)(2,1)S(1)} %collective-permute-done.halo), custom_call_target="tpu_custom_call" | custom-call | flops 17179869184 | bytes 1048576 | tf_op jit(solution)/shard_map/pallas_call | solution.py:292
  9.4 0.0 collective-permute-done.1.tiles
  9.4 0.0 copy-start.2
  9.5 0.0 copy-start.3
  9.5 0.0 copy-start.4
  9.5 0.9 %shard_map.151 = bf16[512,256]{1,0:T(8,128)(2,1)S(1)} custom-call(s32[8,128]{1,0:T(8,128)S(4)} %get-tuple-element.12.index, bf16[1536,256]{1,0:T(8,128)(2,1)S(1)} %get-tuple-element.13.blocks, f32[1,256]{1,0:T(1,128)S(1)} %get-tuple-element.14.gain, bf16[32,128,128]{2,1,0:T(8,128)(2,1)S(1)} %collective-permute-done.1.tiles), custom_call_target="tpu_custom_call" | custom-call | flops 268435456 | bytes 1048576 | tf_op jit(solution)/shard_map/pallas_call | solution.py:303
  10.4 0.0 copy-start.1
  10.4 16.0 %all_to_all.10.normed = bf16[16,32,256]{2,1,0:T(8,128)(2,1)S(1)} all-to-all(bf16[16,32,256]{2,1,0:T(8,128)(2,1)S(1)} %bitcast.8), channel_id=1, replica_groups=mesh['snap'=16,'vert'=32] {'snap'}, dimensions={0} | all-to-all | bytes 524288 | tf_op jit(solution)/shard_map/all_to_all | solution.py:314
  26.4 0.0 copy-done.2
  26.4 0.0 copy-done.3
  26.4 0.0 copy-done.4
  26.4 0.0 copy-done.1
  26.4 1.3 %shard_map.152 = bf16[16,32,256]{2,1,0:T(8,128)(2,1)S(1)} custom-call(f32[1,256]{1,0:T(1,128)S(1)} %get-tuple-element.10.gain, bf16[16,32,256]{2,1,0:T(8,128)(2,1)S(1)} %all_to_all.10.normed, bf16[256,512]{1,0:T(8,128)(2,1)S(1)} %copy-done.3, f32[16,256]{1,0:T(8,128)S(1)} %copy-done.4, bf16[256,1024]{1,0:T(8,128)(2,1)S(1)} %copy-done.1, ...), custom_call_target="tpu_custom_call" | custom-call | flops 671088640 | bytes 1310720 | tf_op jit(solution)/shard_map/pallas_call | solution.py:317
  27.7 11.9 %all_to_all.11 = bf16[16,32,256]{2,1,0:T(8,128)(2,1)S(1)} all-to-all(bf16[16,32,256]{2,1,0:T(8,128)(2,1)S(1)} %shard_map.152), channel_id=1, replica_groups=mesh['snap'=16,'vert'=32] {'snap'}, dimensions={0} | all-to-all | bytes 524288 | tf_op jit(solution)/shard_map/all_to_all | solution.py:335
  39.7 0.0 copy-start
  39.7 0.0 collective-permute-start.2
  39.7 2.3 %all_gather.7.pair = bf16[1024,256]{1,0:T(8,128)(2,1)S(1)} all-gather(bf16[512,256]{1,0:T(8,128)(2,1)S(1)} %bitcast.10), channel_id=1, replica_groups={{0,1},{2,3},{4,5},{6,7},{8,9},{10,11},{12,13},{14,15},{16,17},{18,19},{..., dimensions={0}, use_global_device_ids=true | all-gather | bytes 786432 | tf_op jit(solution)/shard_map/all_gather | solution.py:232
  42.0 0.0 copy-done
  42.0 1.4 %shard_map.153 = (bf16[512,256]{1,0:T(8,128)(2,1)S(1)}, bf16[512,256]{1,0:T(8,128)(2,1)}, s32[8,128]{1,0:T(8,128)S(4)}) custom-call(s32[1,32]{1,0:T(1,128)} %pair_left.1, s32[1,32]{1,0:T(1,128)} %pair_right.1, bf16[1024,256]{1,0:T(8,128)(2,1)S(1)} %all_gather.7.pair, bf16[256,256]{1,0:T(8,128)(2,1)S(1)} %copy-done), custom_call_target="tpu_custom_call" | custom-call | flops 67108864 | bytes 1048576 | tf_op jit(solution)/shard_map/pallas_call | solution.py:340
  43.4 3.9 %collective-permute-done.2.halo = bf16[512,256]{1,0:T(8,128)(2,1)S(1)} collective-permute-done((bf16[512,256]{1,0:T(8,128)(2,1)S(1)}, bf16[512,256]{1,0:T(8,128)(2,1)S(1)}, u32[]{:S(2)}, u32[]{:S(2)}) %collective-permute-start.2) | collective-permute-done | bytes 262176 | tf_op jit(solution)/shard_map/ppermute | solution.py:226
  47.3 1.5 %shard_map.154 = bf16[32,128,128]{2,1,0:T(8,128)(2,1)} custom-call(s32[8,128]{1,0:T(8,128)S(4)} %get-tuple-element.16.index, bf16[512,256]{1,0:T(8,128)(2,1)S(1)} %get-tuple-element.17.left, bf16[1024,256]{1,0:T(8,128)(2,1)S(1)} %all_gather.7.pair, bf16[512,256]{1,0:T(8,128)(2,1)S(1)} %collective-permute-done.2.halo), custom_call_target="tpu_custom_call" | custom-call | flops 268435456 | bytes 1048576 | tf_op jit(solution)/shard_map/pallas_call | solution.py:357
Async XLA Ops:
  0.6 8.2 %collective-permute-start = (bf16[512,256]{1,0:T(8,128)(2,1)}, bf16[512,256]{1,0:T(8,128)(2,1)S(1)}, u32[]{:S(2)}, u32[]{:S(2)}) collective-permute-start(bf16[512,256]{1,0:T(8,128)(2,1)} %bitcast.12), channel_id=1, source_target_pairs={{2,0},{4,2},{6,4},{8,6},{10,8},{12,10},{14,12},{16,14},{18,16},{20... | collective-permute-start | bytes 786440 | tf_op jit(solution)/shard_map/ppermute | solution.py:226
  2.9 6.6 %collective-permute-start.1 = (bf16[32,128,128]{2,1,0:T(8,128)(2,1)}, bf16[32,128,128]{2,1,0:T(8,128)(2,1)S(1)}, u32[]{:S(2)}, u32[]{:S(2)}) collective-permute-start(bf16[32,128,128]{2,1,0:T(8,128)(2,1)} %bitcast.16), channel_id=1, source_target_pairs={{0,1},{1,0},{2,3},{3,2},{4,5},{5,4},{6,7},{7,6},{8,9},{9,8},{10,11... | collective-permute-start | bytes 3145736 | tf_op jit(solution)/shard_map/ppermute | solution.py:286
  9.4 17.0 %copy-start.2 = (bf16[1024,256]{1,0:T(8,128)(2,1)S(1)}, bf16[1024,256]{1,0:T(8,128)(2,1)}, u32[]{:S(2)}) copy-start(bf16[1024,256]{1,0:T(8,128)(2,1)} %down.1) | copy-start | bytes 1572868
  9.5 17.0 %copy-start.3 = (bf16[256,512]{1,0:T(8,128)(2,1)S(1)}, bf16[256,512]{1,0:T(8,128)(2,1)}, u32[]{:S(2)}) copy-start(bf16[256,512]{1,0:T(8,128)(2,1)} %mix.1) | copy-start | bytes 786436
  9.5 16.9 %copy-start.4 = (f32[16,256]{1,0:T(8,128)S(1)}, f32[16,256]{1,0:T(8,128)}, u32[]{:S(2)}) copy-start(f32[16,256]{1,0:T(8,128)} %rates.1) | copy-start | bytes 49156
  10.4 16.0 %copy-start.1 = (bf16[256,1024]{1,0:T(8,128)(2,1)S(1)}, bf16[256,1024]{1,0:T(8,128)(2,1)}, u32[]{:S(2)}) copy-start(bf16[256,1024]{1,0:T(8,128)(2,1)} %up.1) | copy-start | bytes 1572868
  39.7 2.3 %copy-start = (bf16[256,256]{1,0:T(8,128)(2,1)S(1)}, bf16[256,256]{1,0:T(8,128)(2,1)}, u32[]{:S(2)}) copy-start(bf16[256,256]{1,0:T(8,128)(2,1)} %link.1) | copy-start | bytes 393220
  39.7 7.6 %collective-permute-start.2 = (bf16[512,256]{1,0:T(8,128)(2,1)S(1)}, bf16[512,256]{1,0:T(8,128)(2,1)S(1)}, u32[]{:S(2)}, u32[]{:S(2)}) collective-permute-start(bf16[512,256]{1,0:T(8,128)(2,1)S(1)} %bitcast.9), channel_id=1, source_target_pairs={{0,2},{2,4},{4,6},{6,8},{8,10},{10,12},{12,14},{14,16},{16,18},{18... | collective-permute-start | bytes 786440 | tf_op jit(solution)/shard_map/ppermute | solution.py:226
